TPU v7x, 256 devices: a whole 4x4x8 slice. The times are simulated.
256 devices in a mesh: light: 64 (over y, x_lo, z), tex: 4 (over x_hi, core).
Axes of the slice: x: 4 (x_hi: 2, x_lo: 2; x = x_hi * 2 + x_lo), y: 4, z: 8, core: 2. Of those that a mesh axis runs over, the one named last changes fastest.
Arguments:
- light_ids: int32 [128], P('light'), may hold values from 0 to 255
- tile_offsets: int32 [128], P('light'), may hold values from 0 to 4095
- light_table: bfloat16 [256, 512], replicated, may hold values from -6 to 6
- hyper_weight: bfloat16 [512, 1179648], P(None, ('light', 'tex')), may hold values from -0.25 to 0.25
- features: bfloat16 [128, 64, 48, 256], P('light', 'tex'), may hold values from -6 to 6
- upstream_grad: bfloat16 [128, 64, 48, 256], P('light', 'tex'), may hold values from -3 to 3
Outputs:
- relit: bfloat16 [128, 64, 48, 256], P('light', 'tex')
- feature_grad: bfloat16 [128, 64, 48, 256], P('light', 'tex')
- hyper_grad: bfloat16 [512, 1179648], P(None, ('light', 'tex'))
All inputs are finite; a program needn't handle non-finite values.
Results may differ from a plain program's by a relative error of at most 0.02.
Values may be sent and summed in bfloat16 or wider, within the bound.
A program may use at most 128 MiB of HBM per device.

v0:
```python
import math

import jax
import jax.numpy as jnp
from jax import lax
from jax.sharding import PartitionSpec as P


def padded_2(block, sides, width):
    for axis, dim in sides:
        count = lax.axis_size(axis)
        forward = [(i, i + 1) for i in range(count - 1)]
        backward = [(target, source) for source, target in forward]
        low = lax.ppermute(
            lax.slice_in_dim(block, block.shape[dim] - width, None, axis=dim), axis, forward
        )
        high = lax.ppermute(lax.slice_in_dim(block, 0, width, axis=dim), axis, backward)
        block = jnp.concatenate([low, block, high], axis=dim)
    return block


def smooth_act(values):
    return values * jax.nn.sigmoid(values)


def smooth_slope(values):
    sig = jax.nn.sigmoid(values)
    return sig * (1.0 + values * (1.0 - sig))


def light_codes(light_ids, tile_offsets, light_table):
    halfway = light_table.shape[1] // 2
    onehot = (
        light_ids[:, None] == jnp.arange(light_table.shape[0], dtype=jnp.int32)[None, :]
    ).astype(jnp.bfloat16)
    looked = jnp.dot(onehot, light_table, preferred_element_type=jnp.float32)
    rates = jnp.exp(-math.log(1000.0) * jnp.arange(halfway, dtype=jnp.float32) / halfway)
    angles = tile_offsets.astype(jnp.float32)[:, None] * rates[None, :]
    summed = looked + jnp.concatenate([jnp.sin(angles), jnp.cos(angles)], axis=1)
    return (summed * lax.rsqrt(jnp.mean(summed * summed, axis=1, keepdims=True) + 1e-06)).astype(
        jnp.bfloat16
    )


def build_patches(padded, out_rows):
    columns = padded.shape[2]
    wide = jnp.pad(padded, ((0, 0), (0, 0), (1, 1), (0, 0)))
    pieces = [
        wide[:, row_tap : row_tap + out_rows, col_tap : col_tap + columns, :]
        for row_tap in range(3)
        for col_tap in range(3)
    ]
    return jnp.concatenate(pieces, axis=3)


def apply_conv(patches, kernel):
    return jnp.einsum("lrck,lko->lrco", patches, kernel, preferred_element_type=jnp.float32)


def kernel_grad(patches, upstream):
    return jnp.einsum("lrck,lrco->lko", patches, upstream, preferred_element_type=jnp.float32)


def flipped(kernel):
    lights_here, depth, channels = kernel.shape
    shaped = kernel.reshape(lights_here, 3, 3, channels, channels)
    return shaped[:, ::-1, ::-1].swapaxes(3, 4).reshape(lights_here, depth, channels)


def shards(light_ids, tile_offsets, light_table, hyper_weight, features, upstream_grad):
    lights_dev, rows_dev, channels = (features.shape[0], features.shape[1], features.shape[3])
    scale = 1.0 / math.sqrt(9 * channels)
    kernel_len = 9 * channels * channels
    own_codes = light_codes(light_ids, tile_offsets, light_table)
    all_codes = lax.all_gather(own_codes, "light", axis=0, tiled=True)
    columns = (scale * jnp.dot(all_codes, hyper_weight, preferred_element_type=jnp.float32)).astype(
        jnp.bfloat16
    )
    quarters = lax.all_gather(columns, "tex", axis=1, tiled=True)
    weights = lax.all_to_all(quarters, "light", split_axis=0, concat_axis=1, tiled=True)
    first_kernel = weights[:, :kernel_len].reshape(lights_dev, 9 * channels, channels)
    second_kernel = weights[:, kernel_len:].reshape(lights_dev, 9 * channels, channels)
    padded_in = padded_2(features, (("tex", 1),), 1)
    input_patches = build_patches(padded_in, rows_dev)
    first_pre = apply_conv(input_patches, first_kernel)
    hidden = smooth_act(first_pre).astype(jnp.bfloat16)
    padded_hidden = padded_2(hidden, (("tex", 1),), 1)
    hidden_patches = build_patches(padded_hidden, rows_dev)
    second_pre = apply_conv(hidden_patches, second_kernel)
    relit = smooth_act(second_pre).astype(jnp.bfloat16)
    second_grad = (upstream_grad * smooth_slope(second_pre)).astype(jnp.bfloat16)
    padded_grad = padded_2(second_grad, (("tex", 1),), 1)
    hidden_grad = apply_conv(build_patches(padded_grad, rows_dev), flipped(second_kernel))
    first_grad = (hidden_grad * smooth_slope(first_pre)).astype(jnp.bfloat16)
    padded_first = padded_2(first_grad, (("tex", 1),), 1)
    feature_grad = apply_conv(build_patches(padded_first, rows_dev), flipped(first_kernel)).astype(
        jnp.bfloat16
    )
    first_kgrad = kernel_grad(input_patches, first_grad)
    second_kgrad = kernel_grad(hidden_patches, second_grad)
    grads = jnp.concatenate(
        [first_kgrad.reshape(lights_dev, -1), second_kgrad.reshape(lights_dev, -1)], axis=1
    )
    spread = lax.all_to_all(
        grads.astype(jnp.bfloat16), "light", split_axis=1, concat_axis=0, tiled=True
    ).astype(grads.dtype)
    summed = lax.psum_scatter(spread.astype(jnp.bfloat16), "tex", scatter_dimension=1, tiled=True)
    hyper_grad = (
        scale * jnp.einsum("lz,ls->zs", all_codes, summed, preferred_element_type=jnp.float32)
    ).astype(jnp.bfloat16)
    return (relit, feature_grad, hyper_grad)


def solution(mesh):
    in_specs = (
        P("light"),
        P("light"),
        P(),
        P(None, ("light", "tex")),
        P("light", "tex", None, None),
        P("light", "tex", None, None),
    )
    out_specs = (
        P("light", "tex", None, None),
        P("light", "tex", None, None),
        P(None, ("light", "tex")),
    )
    return jax.shard_map(shards, mesh=mesh, in_specs=in_specs, out_specs=out_specs, check_vma=False)
```

profile of v0, /device:TPU:1, one launch (start us, length us, event | category | flops | bytes accessed | tf_op | source)
XLA Modules:
  0.0 607.9 jit_solution(14286666769212236578)
XLA Ops:
  8.1 1.0 multiply_reduce_fusion
  9.2 132.7 %all-gather = bf16[64,2,512]{2,1,0:T(2,128)(2,1)S(1)} all-gather(bf16[1,2,512]{2,1,0:T(2,128)(2,1)S(1)} %fusion.21), channel_id=1, replica_groups=mesh['light'=64,'tex'=4] {'light'}, dimensions={0}, use_global_device_ids=true | all-gather | bytes 133120 | tf_op jit(solution)/shard_map/all_gather | solution.py:75
  141.9 4.1 fusion
  146.1 65.8 %all-gather.3.cloned.1.call-done = bf16[128,18432]{1,0:T(8,128)(2,1)} async-done(((bf16[128,4608]{1,0:T(8,128)(2,1)}), bf16[128,18432]{1,0:T(8,128)(2,1)}) %all-gather.3.cloned.1.call-update) | async-done | bytes 4718608 | tf_op jit(solution)/shard_map/all_gather | solution.py:79
  212.0 7.9 %all_to_all.26 = bf16[64,2,18432]{2,1,0:T(2,128)(2,1)} reshape(bf16[128,18432]{1,0:T(8,128)(2,1)} %all-gather.3.cloned.1.call-done) | data formatting | bytes 9437184 | tf_op jit(solution)/shard_map/all_to_all | solution.py:80
  219.9 10.6 %all-to-all-start = ((bf16[64,2,18432]{2,1,0:T(2,128)(2,1)}), bf16[64,2,18432]{2,1,0:T(2,128)(2,1)}, u32[]{:S(2)}, u32[]{:S(2)}) async-start(bf16[64,2,18432]{2,1,0:T(2,128)(2,1)} %all_to_all.26), calls=%async_computation | async-start | bytes 9437184 | tf_op jit(solution)/shard_map/all_to_all | solution.py:80
  230.5 4.1 collective-permute-start
  234.7 1.9 collective-permute-start.1
  236.6 4.8 collective-permute-done
  241.4 3.0 collective-permute-done.1
  245.0 1.0 slice_dynamic-update-slice_fusion.23
  246.1 1.1 fusion.18
  247.1 1.3 slice_dynamic-update-slice_fusion.22
  248.4 1.0 slice_dynamic-update-slice_fusion.21
  249.4 1.0 constant_dynamic-update-slice_fusion
  250.4 1.4 slice_dynamic-update-slice_fusion.20
  251.8 1.0 slice_dynamic-update-slice_fusion.19
  252.7 1.0 fusion.17
  253.8 1.3 slice_dynamic-update-slice_fusion.18
  255.1 77.5 %all-to-all-done = bf16[64,2,18432]{2,1,0:T(2,128)(2,1)} async-done(((bf16[64,2,18432]{2,1,0:T(2,128)(2,1)}), bf16[64,2,18432]{2,1,0:T(2,128)(2,1)}, u32[]{:S(2)}, u32[]{:S(2)}) %all-to-all-start) | async-done | bytes 4718624 | tf_op jit(solution)/shard_map/all_to_all | solution.py:80
  332.6 5.5 fusion.25
  338.1 8.0 %multiply_convert_fusion.4 = (bf16[2,16,48,256]{3,2,1,0:T(8,128)(2,1)S(1)}, f32[2,16,48,256]{3,2,1,0:T(8,128)}) fusion(bf16[2,16,48,2304]{3,2,1,0:T(8,128)(2,1)} %slice_dynamic-update-slice_fusion.18, bf16[1,2,2304,256]{3,1,2,0:T(2,128)(2,1)S(1)} %bitcast.80), kind=kOutput, calls=%fused_computation.19 | convolution fusion | flops 1813905408 | bytes 11796480 | tf_op jit(solution)/shard_map/lrck,lko->lrco/dot_general | solution.py:57
  346.2 10.2 %collective-permute-start.2 = (bf16[2,1,48,256]{3,2,1,0:T(8,128)(2,1)S(1)}, bf16[2,1,48,256]{3,2,1,0:T(8,128)(2,1)S(1)}, u32[]{:S(2)}, u32[]{:S(2)}) collective-permute-start(bf16[2,1,48,256]{3,2,1,0:T(8,128)(2,1)S(1)} %get-tuple-element.11), channel_id=1, source_target_pairs={{0,1},{1,2},{2,3},{4,5},{5,6},{6,7},{8,9},{9,10},{10,11},{12,13},{... | collective-permute-start | bytes 147464 | tf_op jit(solution)/shard_map/ppermute | solution.py:14
  356.4 2.4 collective-permute-start.3
  358.8 1.7 copy.26
  360.6 2.8 copy.15
  363.4 1.6 rev.6
  367.9 3.4 multiply_convert_fusion.2
  371.4 5.1 collective-permute-start.4
  376.5 1.9 collective-permute-start.5
  378.4 4.4 fusion.2
  382.9 3.2 concatenate.78
  386.0 3.8 copy.18
  393.1 2.3 multiply_convert_fusion.1
  395.4 7.3 %fusion.1 = bf16[2,2304,256]{2,1,0:T(8,128)(2,1)} fusion(bf16[2,16,48,2304]{3,2,1,0:T(8,128)(2,1)} %slice_dynamic-update-slice_fusion.18, bf16[2,16,48,256]{3,2,1,0:T(8,128)(2,1)S(1)} %multiply_convert_fusion.1), kind=kOutput, calls=%fused_computation.6 | convolution fusion | flops 1813118976 | bytes 10223616 | tf_op jit(solution)/shard_map/lrck,lrco->lko/dot_general | solution.py:61
  402.6 3.2 concatenate.77
  405.9 3.9 copy.17
  409.7 10.6 %pad_maximum_fusion = bf16[2,64,18432]{2,0,1:T(2,128)(2,1)} fusion(bf16[2,32,18432]{2,0,1:T(2,128)(2,1)} %copy.18, bf16[2,32,18432]{2,0,1:T(2,128)(2,1)} %copy.17), kind=kLoop, calls=%fused_computation.5 | loop fusion | flops 2359296 | bytes 9437184 | tf_op jit(solution)/shard_map/concatenate | solution.py:101
  420.4 111.9 %all_to_all.35 = bf16[2,64,18432]{2,0,1:T(2,128)(2,1)} all-to-all(bf16[2,64,18432]{2,0,1:T(2,128)(2,1)} %pad_maximum_fusion), channel_id=1, replica_groups=mesh['light'=64,'tex'=4] {'light'}, dimensions={1} | all-to-all | bytes 9437184 | tf_op jit(solution)/shard_map/all_to_all | solution.py:104
  532.2 7.5 %all_to_all.32 = bf16[128,18432]{1,0:T(8,128)(2,1)} reshape(bf16[64,2,18432]{2,1,0:T(2,128)(2,1)} %bitcast.77) | data formatting | bytes 9437184 | tf_op jit(solution)/shard_map/all_to_all | solution.py:104
  539.8 5.4 collective-permute-start.6
  545.2 1.9 collective-permute-start.7
  547.1 2.0 copy.25
  549.2 2.7 copy.16
  551.9 1.9 rev.7
  556.0 2.9 convolution_convert_fusion
  558.9 37.0 %reduce-scatter.2.cloned.1.call-done = bf16[128,4608]{1,0:T(8,128)(2,1)} async-done(((bf16[128,18432]{1,0:T(8,128)(2,1)}), bf16[128,4608]{1,0:T(8,128)(2,1)}) %reduce-scatter.2.cloned.1.call-update) | async-done | bytes 1179664 | tf_op jit(solution)/shard_map/reduce_scatter | solution.py:107
  595.9 4.9 multiply_convert_fusion
  (69 shorter events, 9.8 us)
Async XLA Ops:
  7.2 1.0 copy-start
  7.2 204.8 %all-gather.3.cloned.1.call-start = ((), (), s32[]{:S(2)}) async-start(), calls=%async_computation.3 | async-start | bytes 5898240 | tf_op jit(solution)/shard_map/all_gather | solution.py:79
  219.9 10.6 %copy-start.2 = (bf16[2,16,48,256]{3,2,1,0:T(8,128)(2,1)S(1)}, bf16[2,16,48,256]{3,2,1,0:T(8,128)(2,1)}, u32[]{:S(2)}) copy-start(bf16[2,16,48,256]{3,2,1,0:T(8,128)(2,1)} %param.10) | copy-start | bytes 2359300
  219.9 112.7 %all-to-all-start = ((bf16[64,2,18432]{2,1,0:T(2,128)(2,1)}), bf16[64,2,18432]{2,1,0:T(2,128)(2,1)}, u32[]{:S(2)}, u32[]{:S(2)}) async-start(bf16[64,2,18432]{2,1,0:T(2,128)(2,1)} %all_to_all.26), calls=%async_computation | async-start | bytes 9437184 | tf_op jit(solution)/shard_map/all_to_all | solution.py:80
  230.5 365.4 %reduce-scatter.2.cloned.1.call-start = ((), (), s32[]{:S(2)}) async-start(), calls=%async_computation.4 | async-start | bytes 5898240 | tf_op jit(solution)/shard_map/reduce_scatter | solution.py:107
  230.5 10.9 %collective-permute-start = (bf16[2,1,48,256]{3,2,1,0:T(8,128)(2,1)S(1)}, bf16[2,1,48,256]{3,2,1,0:T(8,128)(2,1)S(1)}, u32[]{:S(2)}, u32[]{:S(2)}) collective-permute-start(bf16[2,1,48,256]{3,2,1,0:T(8,128)(2,1)S(1)} %get-tuple-element.13), channel_id=1, source_target_pairs={{0,1},{1,2},{2,3},{4,5},{5,6},{6,7},{8,9},{9,10},{10,11},{12,13},{... | collective-permute-start | bytes 147464 | tf_op jit(solution)/shard_map/ppermute | solution.py:14
  234.7 9.8 %collective-permute-start.1 = (bf16[2,1,48,256]{3,2,1,0:T(8,128)(2,1)S(1)}, bf16[2,1,48,256]{3,2,1,0:T(8,128)(2,1)S(1)}, u32[]{:S(2)}, u32[]{:S(2)}) collective-permute-start(bf16[2,1,48,256]{3,2,1,0:T(8,128)(2,1)S(1)} %get-tuple-element.14), channel_id=1, source_target_pairs={{1,0},{2,1},{3,2},{5,4},{6,5},{7,6},{9,8},{10,9},{11,10},{13,12},{... | collective-permute-start | bytes 147464 | tf_op jit(solution)/shard_map/ppermute | solution.py:17
  338.1 8.0 %copy-start.3 = (bf16[2,589824]{1,0:T(2,128)(2,1)}, bf16[2,589824]{1,0:T(2,128)(2,1)S(1)}, u32[]{:S(2)}) copy-start(bf16[2,589824]{1,0:T(2,128)(2,1)S(1)} %get-tuple-element.4) | copy-start | bytes 7077892
  338.1 20.7 %copy-start.4 = (bf16[2,589824]{1,0:T(2,128)(2,1)}, bf16[2,589824]{1,0:T(2,128)(2,1)S(1)}, u32[]{:S(2)}) copy-start(bf16[2,589824]{1,0:T(2,128)(2,1)S(1)} %get-tuple-element.3) | copy-start | bytes 7077892
  346.2 18.8 %collective-permute-start.2 = (bf16[2,1,48,256]{3,2,1,0:T(8,128)(2,1)S(1)}, bf16[2,1,48,256]{3,2,1,0:T(8,128)(2,1)S(1)}, u32[]{:S(2)}, u32[]{:S(2)}) collective-permute-start(bf16[2,1,48,256]{3,2,1,0:T(8,128)(2,1)S(1)} %get-tuple-element.11), channel_id=1, source_target_pairs={{0,1},{1,2},{2,3},{4,5},{5,6},{6,7},{8,9},{9,10},{10,11},{12,13},{... | collective-permute-start | bytes 147464 | tf_op jit(solution)/shard_map/ppermute | solution.py:14
  356.4 8.6 %collective-permute-start.3 = (bf16[2,1,48,256]{3,2,1,0:T(8,128)(2,1)S(1)}, bf16[2,1,48,256]{3,2,1,0:T(8,128)(2,1)S(1)}, u32[]{:S(2)}, u32[]{:S(2)}) collective-permute-start(bf16[2,1,48,256]{3,2,1,0:T(8,128)(2,1)S(1)} %get-tuple-element.12), channel_id=1, source_target_pairs={{1,0},{2,1},{3,2},{5,4},{6,5},{7,6},{9,8},{10,9},{11,10},{13,12},{... | collective-permute-start | bytes 147464 | tf_op jit(solution)/shard_map/ppermute | solution.py:17
  366.1 1.7 copy-start.5
  366.1 1.8 copy-start.7
  371.4 18.5 %collective-permute-start.4 = (bf16[2,1,48,256]{3,2,1,0:T(8,128)(2,1)S(1)}, bf16[2,1,48,256]{3,2,1,0:T(8,128)(2,1)S(1)}, u32[]{:S(2)}, u32[]{:S(2)}) collective-permute-start(bf16[2,1,48,256]{3,2,1,0:T(8,128)(2,1)S(1)} %get-tuple-element.9), channel_id=1, source_target_pairs={{0,1},{1,2},{2,3},{4,5},{5,6},{6,7},{8,9},{9,10},{10,11},{12,13},{... | collective-permute-start | bytes 147464 | tf_op jit(solution)/shard_map/ppermute | solution.py:14
  376.5 13.4 %collective-permute-start.5 = (bf16[2,1,48,256]{3,2,1,0:T(8,128)(2,1)S(1)}, bf16[2,1,48,256]{3,2,1,0:T(8,128)(2,1)S(1)}, u32[]{:S(2)}, u32[]{:S(2)}) collective-permute-start(bf16[2,1,48,256]{3,2,1,0:T(8,128)(2,1)S(1)} %get-tuple-element.10), channel_id=1, source_target_pairs={{1,0},{2,1},{3,2},{5,4},{6,5},{7,6},{9,8},{10,9},{11,10},{13,12},{... | collective-permute-start | bytes 147464 | tf_op jit(solution)/shard_map/ppermute | solution.py:17
  390.9 1.7 copy-start.6
  391.0 2.1 copy-start.8
  539.8 14.1 %collective-permute-start.6 = (bf16[2,1,48,256]{3,2,1,0:T(8,128)(2,1)S(1)}, bf16[2,1,48,256]{3,2,1,0:T(8,128)(2,1)S(1)}, u32[]{:S(2)}, u32[]{:S(2)}) collective-permute-start(bf16[2,1,48,256]{3,2,1,0:T(8,128)(2,1)S(1)} %get-tuple-element.7), channel_id=1, source_target_pairs={{0,1},{1,2},{2,3},{4,5},{5,6},{6,7},{8,9},{9,10},{10,11},{12,13},{... | collective-permute-start | bytes 147464 | tf_op jit(solution)/shard_map/ppermute | solution.py:14
  545.2 8.6 %collective-permute-start.7 = (bf16[2,1,48,256]{3,2,1,0:T(8,128)(2,1)S(1)}, bf16[2,1,48,256]{3,2,1,0:T(8,128)(2,1)S(1)}, u32[]{:S(2)}, u32[]{:S(2)}) collective-permute-start(bf16[2,1,48,256]{3,2,1,0:T(8,128)(2,1)S(1)} %get-tuple-element.8), channel_id=1, source_target_pairs={{1,0},{2,1},{3,2},{5,4},{6,5},{7,6},{9,8},{10,9},{11,10},{13,12},{... | collective-permute-start | bytes 147464 | tf_op jit(solution)/shard_map/ppermute | solution.py:17
  556.0 44.8 %copy-start.1 = (bf16[256,512]{1,0:T(8,128)(2,1)S(1)}, bf16[256,512]{1,0:T(8,128)(2,1)}, u32[]{:S(2)}) copy-start(bf16[256,512]{1,0:T(8,128)(2,1)} %param.8) | copy-start | bytes 786436
Sparse Core Ops, SparseCore 0:
  146.2 65.6 all-gather.2
  539.9 55.9 reduce-scatter.1
where the time goes:
time: 615 us; the launch traced here: 608 us
  blocking collectives  245 us (40%)
  waiting for transfers between devices  188 us (31%)
  local copies, waits for them, and re-layouts  62 us (10%)
  starting transfers between devices  43.7 us (7%)
  matrix products  38.3 us (6%)
  other arithmetic  16.2 us (3%)
  between operations  14.8 us (2%)
    all_gather x1, blocking collectives, shards(): all_codes = lax.all_gather(own_codes, 'light', axis=0, tiled=True)  133 us
    all_to_all x1, blocking collectives, shards(): lax.all_to_all(grads.astype(jnp.bfloat16), 'light', split_axis=1, concat_...  112 us
    all_to_all x1, waiting for transfers between devices, shards(): lax.all_to_all(quarters, 'light', split_axis=0, concat_axis=1, tiled=True)  77.5 us
    all_gather x1, waiting for transfers between devices, shards(): quarters = lax.all_gather(columns, 'tex', axis=1, tiled=True)  65.8 us
    reduce_scatter x1, waiting for transfers between devices, shards(): lax.psum_scatter(spread.astype(jnp.bfloat16), 'tex', scatter_dimension=1,...  37 us
    ppermute x4, starting transfers between devices, padded_2(): lax.ppermute(lax.slice_in_dim(block, block.shape[dim] - width, None, axis...  24.9 us
    dot_general x4, matrix products, apply_conv(): jnp.einsum('lrck,lko->lrco', patches, kernel, preferred_element_type=jnp....  16.6 us
    unnamed x45, local copies, waits for them, and re-layouts  15.4 us
  transfers between devices with their start and end apart: 11, of which 5 were waited for; matrix products, arithmetic and copies ran while one was open for 7% of the time, Pallas kernels for 0%

commit v1 on v0

--- a/solution.py
+++ b/solution.py
@@ -72,12 +72,21 @@
     scale = 1.0 / math.sqrt(9 * channels)
     kernel_len = 9 * channels * channels
     own_codes = light_codes(light_ids, tile_offsets, light_table)
-    all_codes = lax.all_gather(own_codes, "light", axis=0, tiled=True)
+    devices = lax.axis_size("light")
+    quarters = lax.axis_size("tex")
+    own_len = hyper_weight.shape[1]
+    copies = jnp.broadcast_to(own_codes[None], (devices,) + own_codes.shape)
+    all_codes = lax.all_to_all(copies, "light", split_axis=0, concat_axis=0, tiled=True).reshape(
+        devices * lights_dev, -1
+    )
     columns = (scale * jnp.dot(all_codes, hyper_weight, preferred_element_type=jnp.float32)).astype(
         jnp.bfloat16
     )
-    quarters = lax.all_gather(columns, "tex", axis=1, tiled=True)
-    weights = lax.all_to_all(quarters, "light", split_axis=0, concat_axis=1, tiled=True)
+    mine = lax.all_to_all(
+        columns.reshape(devices, lights_dev, own_len), "light", split_axis=0, concat_axis=0, tiled=True
+    )
+    weights = lax.all_gather(mine, "tex", axis=0)
+    weights = weights.transpose(2, 1, 0, 3).reshape(lights_dev, 2 * kernel_len)
     first_kernel = weights[:, :kernel_len].reshape(lights_dev, 9 * channels, channels)
     second_kernel = weights[:, kernel_len:].reshape(lights_dev, 9 * channels, channels)
     padded_in = padded_2(features, (("tex", 1),), 1)
@@ -101,10 +110,13 @@
     grads = jnp.concatenate(
         [first_kgrad.reshape(lights_dev, -1), second_kgrad.reshape(lights_dev, -1)], axis=1
     )
-    spread = lax.all_to_all(
-        grads.astype(jnp.bfloat16), "light", split_axis=1, concat_axis=0, tiled=True
-    ).astype(grads.dtype)
-    summed = lax.psum_scatter(spread.astype(jnp.bfloat16), "tex", scatter_dimension=1, tiled=True)
+    blocks = grads.astype(jnp.bfloat16).reshape(lights_dev, devices, quarters, own_len)
+    mixed = lax.psum_scatter(
+        blocks.transpose(2, 1, 0, 3), "tex", scatter_dimension=0, tiled=False
+    )
+    summed = lax.all_to_all(mixed, "light", split_axis=0, concat_axis=0, tiled=True).reshape(
+        devices * lights_dev, own_len
+    )
     hyper_grad = (
         scale * jnp.einsum("lz,ls->zs", all_codes, summed, preferred_element_type=jnp.float32)
     ).astype(jnp.bfloat16)

time: 615 us -> 320 us (0.52)
  blocking collectives: 245 us -> 55.3 us
  waiting for transfers between devices: 188 us -> 82.6 us
  local copies, waits for them, and re-layouts: 62 us -> 71.7 us
  other arithmetic: 16.2 us -> 9.87 us
    all_gather x1 -> x0, blocking collectives: 133 us -> none  [shards(): all_codes = lax.all_gather(own_codes, 'light', axis=0, tiled=True)]
    all_to_all x1, waiting for transfers between devices: 77.5 us -> 14.9 us  [shards(): lax.all_to_all(mixed, 'light', split_axis=0, concat_axis=0, tiled=True)]
    all_to_all x1 -> x2, blocking collectives: 112 us -> 55.3 us  [the longest x1 31.9 us: shards(): lax.all_to_all(columns.reshape(devices, lights_dev, own_len), 'light', sp...]
    all_gather x1, waiting for transfers between devices: 65.8 us -> 18.7 us  [shards(): weights = lax.all_gather(mine, 'tex', axis=0)]
    all_to_all x2 -> x0, local copies, waits for them, and re-layouts: 15.4 us -> none  [the longest x1 7.95 us: shards(): lax.all_to_all(quarters, 'light', split_axis=0, concat_axis=1, tiled=True)]
    concatenate x1 -> x0, other arithmetic: 10.6 us -> none  [shards(): jnp.concatenate([first_kgrad.reshape(lights_dev, -1), second_kgrad.reshap...]
    transpose x0 -> x1, local copies, waits for them, and re-layouts: none -> 8.16 us  [shards(): weights = weights.transpose(2, 1, 0, 3).reshape(lights_dev, 2 * kernel_len)]
    reduce_scatter x1, waiting for transfers between devices: 37 us -> 44.3 us  [shards(): lax.psum_scatter(blocks.transpose(2, 1, 0, 3), 'tex', scatter_dimension=0...]
  transfers between devices with their start and end apart: 11 -> 11, of which waited for: 5 -> 4; matrix products, arithmetic and copies ran while one was open for 7% -> 17% of each run, Pallas kernels for 0% -> 0%
where the time goes in v1:
time: 320 us; the launch traced here: 314 us
  waiting for transfers between devices  82.6 us (26%)
  local copies, waits for them, and re-layouts  71.7 us (22%)
  blocking collectives  55.3 us (17%)
  starting transfers between devices  40.7 us (13%)
  matrix products  39.1 us (12%)
  between operations  14.7 us (5%)
  other arithmetic  9.87 us (3%)
    reduce_scatter x1, waiting for transfers between devices, shards(): lax.psum_scatter(blocks.transpose(2, 1, 0, 3), 'tex', scatter_dimension=0...  44.3 us
    all_to_all x1, blocking collectives, shards(): lax.all_to_all(columns.reshape(devices, lights_dev, own_len), 'light', sp...  31.9 us
    all_to_all x1, blocking collectives, shards(): lax.all_to_all(copies, 'light', split_axis=0, concat_axis=0, tiled=True)  23.4 us
    unnamed x48, local copies, waits for them, and re-layouts  22.2 us
    ppermute x4, starting transfers between devices, padded_2(): lax.ppermute(lax.slice_in_dim(block, block.shape[dim] - width, None, axis...  21.6 us
    dot_general x4, matrix products, apply_conv(): jnp.einsum('lrck,lko->lrco', patches, kernel, preferred_element_type=jnp....  19.7 us
    all_gather x1, waiting for transfers between devices, shards(): weights = lax.all_gather(mine, 'tex', axis=0)  18.7 us
    all_to_all x1, waiting for transfers between devices, shards(): lax.all_to_all(mixed, 'light', split_axis=0, concat_axis=0, tiled=True)  14.9 us
  transfers between devices with their start and end apart: 11, of which 4 were waited for; matrix products, arithmetic and copies ran while one was open for 17% of the time, Pallas kernels for 0%

profile of v1, /device:TPU:1, one launch (start us, length us, event | category | flops | bytes accessed | tf_op | source)
XLA Modules:
  0.0 314.0 jit_solution(16016403001158973718)
XLA Ops:
  9.2 23.4 %all_to_all.15 = bf16[64,2,512]{2,1,0:T(2,128)(2,1)S(1)} all-to-all(bf16[64,2,512]{2,1,0:T(2,128)(2,1)S(1)} %broadcast_in_dim.2), channel_id=1, replica_groups=mesh['light'=64,'tex'=4] {'light'}, dimensions={0} | all-to-all | bytes 262144 | tf_op jit(solution)/shard_map/all_to_all | solution.py:79
  32.7 3.2 %fusion.1 = bf16[128,4608]{1,0:T(8,128)(2,1)S(1)} fusion(bf16[128,512]{1,0:T(8,128)(2,1)S(1)} %reshape.53, bf16[512,4608]{1,0:T(8,128)(2,1)} %param.9), kind=kOutput, calls=%fused_computation.3 | convolution fusion | flops 605159424 | bytes 6029312 | tf_op jit(solution)/shard_map/dot_general | solution.py:82
  36.4 31.9 %all_to_all.16 = bf16[64,2,4608]{2,1,0:T(2,128)(2,1)} all-to-all(bf16[64,2,4608]{2,1,0:T(2,128)(2,1)S(1)} %reshape.54), channel_id=1, replica_groups=mesh['light'=64,'tex'=4] {'light'}, dimensions={0} | all-to-all | bytes 2359296 | tf_op jit(solution)/shard_map/all_to_all | solution.py:85
  68.4 9.6 %collective-permute-start = (bf16[2,1,48,256]{3,2,1,0:T(8,128)(2,1)S(1)}, bf16[2,1,48,256]{3,2,1,0:T(8,128)(2,1)S(1)}, u32[]{:S(2)}, u32[]{:S(2)}) collective-permute-start(bf16[2,1,48,256]{3,2,1,0:T(8,128)(2,1)S(1)} %get-tuple-element.13), channel_id=1, source_target_pairs={{0,1},{1,2},{2,3},{4,5},{5,6},{6,7},{8,9},{9,10},{10,11},{12,13},{... | collective-permute-start | bytes 147464 | tf_op jit(solution)/shard_map/ppermute | solution.py:14
  78.0 2.2 collective-permute-start.1
  80.2 4.7 %collective-permute-done.1 = bf16[2,1,48,256]{3,2,1,0:T(8,128)(2,1)S(1)} collective-permute-done((bf16[2,1,48,256]{3,2,1,0:T(8,128)(2,1)S(1)}, bf16[2,1,48,256]{3,2,1,0:T(8,128)(2,1)S(1)}, u32[]{:S(2)}, u32[]{:S(2)}) %collective-permute-start.1) | collective-permute-done | bytes 49184 | tf_op jit(solution)/shard_map/ppermute | solution.py:17
  86.5 1.0 fusion.20
  87.5 1.4 slice_dynamic-update-slice_fusion.22
  90.8 1.3 slice_dynamic-update-slice_fusion.20
  92.2 1.0 slice_dynamic-update-slice_fusion.19
  94.1 1.4 slice_dynamic-update-slice_fusion.18
  95.5 18.7 %all-gather.3.cloned.1.call-done = bf16[256,2,4608]{2,1,0:T(2,128)(2,1)} async-done(((bf16[64,2,4608]{2,1,0:T(2,128)(2,1)}), bf16[256,2,4608]{2,1,0:T(2,128)(2,1)}) %all-gather.3.cloned.1.call-update) | async-done | bytes 4718608 | tf_op jit(solution)/shard_map/all_gather | solution.py:88
  114.2 8.2 %copy.27 = bf16[2,64,4,4608]{3,2,1,0:T(4,128)(2,1)} copy(bf16[2,64,4,4608]{3,0,1,2:T(2,128)(2,1)} %bitcast.85) | data formatting | bytes 9437184 | tf_op jit(solution)/shard_map/transpose | solution.py:89
  122.3 6.3 %reshape.55 = bf16[2,1179648]{1,0:T(2,128)(2,1)} reshape(bf16[2,64,4,4608]{3,2,1,0:T(4,128)(2,1)} %copy.27) | data formatting | bytes 9437184 | tf_op jit(solution)/shard_map/reshape | solution.py:89
  128.6 5.5 %fusion.27 = (bf16[2,589824]{1,0:T(2,128)(2,1)S(1)}, bf16[2,589824]{1,0:T(2,128)(2,1)S(1)}) fusion(bf16[2,1179648]{1,0:T(2,128)(2,1)} %reshape.55), kind=kLoop, calls=%fused_computation.92 | loop fusion | bytes 9437184 | tf_op jit(solution)/shard_map/slice | solution.py:91
  134.1 8.1 %multiply_convert_fusion.3 = (bf16[2,16,48,256]{3,2,1,0:T(8,128)(2,1)S(1)}, f32[2,16,48,256]{3,2,1,0:T(8,128)}) fusion(bf16[2,16,48,2304]{3,2,1,0:T(8,128)(2,1)} %slice_dynamic-update-slice_fusion.18, bf16[1,2,2304,256]{3,1,2,0:T(2,128)(2,1)S(1)} %bitcast.81), kind=kOutput, calls=%fused_computation.20 | convolution fusion | flops 1813905408 | bytes 11796480 | tf_op jit(solution)/shard_map/lrck,lko->lrco/dot_general | solution.py:57
  142.2 2.1 collective-permute-start.2
  144.3 2.8 collective-permute-start.3
  147.1 1.7 copy.42
  148.8 2.8 copy.28
  151.7 1.5 rev.6
  156.1 3.4 %multiply_convert_fusion.1 = (bf16[2,16,48,256]{3,2,1,0:T(8,128)(2,1)S(1)}, bf16[2,16,48,256]{3,2,1,0:T(8,128)(2,1)}) fusion(bf16[2,16,48,256]{3,2,1,0:T(8,128)(2,1)S(1)} %copy-done.9, bf16[2,16,48,2304]{3,2,1,0:T(8,128)(2,1)S(1)} %slice_dynamic-update-slice_fusion.12, bf16[1,2,2304,256]{3,1,2,0:T(2,128)(2,1)S(1)} %bitcast.84), kind=kOutput, calls=%fused_computation.17 | convolution fusion | flops 1816657920 | bytes 11796480 | tf_op jit(solution)/shard_map/lrck,lko->lrco/dot_general | solution.py:57
  159.5 4.8 %collective-permute-start.4 = (bf16[2,1,48,256]{3,2,1,0:T(8,128)(2,1)S(1)}, bf16[2,1,48,256]{3,2,1,0:T(8,128)(2,1)S(1)}, u32[]{:S(2)}, u32[]{:S(2)}) collective-permute-start(bf16[2,1,48,256]{3,2,1,0:T(8,128)(2,1)S(1)} %get-tuple-element.9), channel_id=1, source_target_pairs={{0,1},{1,2},{2,3},{4,5},{5,6},{6,7},{8,9},{9,10},{10,11},{12,13},{... | collective-permute-start | bytes 147464 | tf_op jit(solution)/shard_map/ppermute | solution.py:14
  164.4 1.9 collective-permute-start.5
  166.3 4.4 %fusion.3 = bf16[2,2304,256]{2,1,0:T(8,128)(2,1)} fusion(bf16[2,16,48,2304]{3,2,1,0:T(8,128)(2,1)S(1)} %slice_dynamic-update-slice_fusion.12, bf16[2,16,48,256]{3,2,1,0:T(8,128)(2,1)S(1)} %get-tuple-element.5), kind=kOutput, calls=%fused_computation.8 | convolution fusion | flops 1813118976 | bytes 10223616 | tf_op jit(solution)/shard_map/lrck,lrco->lko/dot_general | solution.py:61
  170.7 4.6 %concatenate.78 = bf16[2,32,4,4608]{3,2,1,0:T(4,128)(2,1)S(1)} reshape(bf16[2,2304,256]{2,1,0:T(8,128)(2,1)} %fusion.3) | data formatting | bytes 4718592 | tf_op jit(solution)/shard_map/concatenate | solution.py:110
  175.3 1.8 copy.31
  180.4 2.3 multiply_convert_fusion
  182.7 7.3 %fusion.2 = bf16[2,2304,256]{2,1,0:T(8,128)(2,1)} fusion(bf16[2,16,48,2304]{3,2,1,0:T(8,128)(2,1)} %slice_dynamic-update-slice_fusion.18, bf16[2,16,48,256]{3,2,1,0:T(8,128)(2,1)S(1)} %multiply_convert_fusion), kind=kOutput, calls=%fused_computation.7 | convolution fusion | flops 1813118976 | bytes 10223616 | tf_op jit(solution)/shard_map/lrck,lrco->lko/dot_general | solution.py:61
  189.9 4.4 %concatenate.77 = bf16[2,32,4,4608]{3,2,1,0:T(4,128)(2,1)S(1)} reshape(bf16[2,2304,256]{2,1,0:T(8,128)(2,1)} %fusion.2) | data formatting | bytes 4718592 | tf_op jit(solution)/shard_map/concatenate | solution.py:110
  194.8 1.3 copy-done.6
  196.0 2.5 maximum_bitcast_fusion
  198.6 5.1 %collective-permute-start.6 = (bf16[2,1,48,256]{3,2,1,0:T(8,128)(2,1)S(1)}, bf16[2,1,48,256]{3,2,1,0:T(8,128)(2,1)S(1)}, u32[]{:S(2)}, u32[]{:S(2)}) collective-permute-start(bf16[2,1,48,256]{3,2,1,0:T(8,128)(2,1)S(1)} %get-tuple-element.7), channel_id=1, source_target_pairs={{0,1},{1,2},{2,3},{4,5},{5,6},{6,7},{8,9},{9,10},{10,11},{12,13},{... | collective-permute-start | bytes 147464 | tf_op jit(solution)/shard_map/ppermute | solution.py:14
  203.7 1.9 collective-permute-start.7
  205.6 2.0 copy.41
  207.6 2.7 copy.29
  210.3 3.6 %rev.7 = bf16[2,3,3,256,256]{3,4,2,1,0:T(8,128)(2,1)} reverse(bf16[2,3,3,256,256]{3,4,2,1,0:T(8,128)(2,1)} %copy.29), dimensions={1,2} | reverse | bytes 4718592 | tf_op jit(solution)/shard_map/rev | solution.py:67
  215.4 1.0 fusion.14
  216.4 44.3 %reduce-scatter.2.cloned.1.call-done = bf16[1,64,2,4608]{3,1,2,0:T(8,128)(2,1)} async-done(((bf16[4,64,2,4608]{3,1,2,0:T(8,128)(2,1)}), bf16[1,64,2,4608]{3,1,2,0:T(8,128)(2,1)}) %reduce-scatter.2.cloned.1.call-update) | async-done | bytes 1179664 | tf_op jit(solution)/shard_map/reduce_scatter | solution.py:114
  260.7 3.5 %copy.32 = bf16[64,2,4608]{2,1,0:T(2,128)(2,1)} copy(bf16[64,2,4608]{2,0,1:T(8,128)(2,1)} %bitcast.88) | data formatting | bytes 2359296 | tf_op jit(solution)/shard_map/reduce_scatter | solution.py:114
  264.2 10.2 %all-to-all-start.2 = ((bf16[64,2,4608]{2,1,0:T(2,128)(2,1)}), bf16[64,2,4608]{2,1,0:T(2,128)(2,1)S(1)}, u32[]{:S(2)}, u32[]{:S(2)}) async-start(bf16[64,2,4608]{2,1,0:T(2,128)(2,1)} %copy.32), calls=%async_computation.3 | async-start | bytes 2359296 | tf_op jit(solution)/shard_map/all_to_all | solution.py:117
  274.4 1.4 slice_dynamic-update-slice_fusion.4
  277.8 1.3 slice_dynamic-update-slice_fusion.2
  279.1 1.0 slice_dynamic-update-slice_fusion.1
  281.1 1.4 slice_dynamic-update-slice_fusion
  282.5 5.9 %convolution_convert_fusion = bf16[2,16,48,256]{3,2,1,0:T(8,128)(2,1)} fusion(bf16[2,16,48,2304]{3,2,1,0:T(8,128)(2,1)} %slice_dynamic-update-slice_fusion, bf16[2,2304,256,1]{2,1,3,0:T(8,128)(2,1)S(1)} %bitcast.87), kind=kOutput, calls=%fused_computation.22 | convolution fusion | flops 1812332544 | bytes 10223616 | tf_op jit(solution)/shard_map/lrck,lko->lrco/dot_general | solution.py:57
  288.4 14.9 %all-to-all-done.2 = bf16[64,2,4608]{2,1,0:T(2,128)(2,1)S(1)} async-done(((bf16[64,2,4608]{2,1,0:T(2,128)(2,1)}), bf16[64,2,4608]{2,1,0:T(2,128)(2,1)S(1)}, u32[]{:S(2)}, u32[]{:S(2)}) %all-to-all-start.2) | async-done | bytes 1179680 | tf_op jit(solution)/shard_map/all_to_all | solution.py:117
  303.3 3.6 %fusion = bf16[512,4608]{1,0:T(8,128)(2,1)} fusion(bf16[64,2,4608]{2,1,0:T(2,128)(2,1)S(1)} %all-to-all-done.2, bf16[64,2,512]{2,1,0:T(2,128)(2,1)S(1)} %all_to_all.15), kind=kOutput, calls=%fused_computation.1 | convolution fusion | flops 608698368 | bytes 6029312 | tf_op jit(solution)/shard_map/lz,ls->zs/dot_general | solution.py:121
  (76 shorter events, 18.0 us)
Async XLA Ops:
  7.2 1.0 copy-start
  7.2 107.0 %all-gather.3.cloned.1.call-start = ((), (), s32[]{:S(2)}) async-start(), calls=%async_computation.5 | async-start | bytes 5898240 | tf_op jit(solution)/shard_map/all_gather | solution.py:88
  32.7 35.7 %copy-start.2 = (bf16[2,16,48,256]{3,2,1,0:T(8,128)(2,1)S(1)}, bf16[2,16,48,256]{3,2,1,0:T(8,128)(2,1)}, u32[]{:S(2)}) copy-start(bf16[2,16,48,256]{3,2,1,0:T(8,128)(2,1)} %param.10) | copy-start | bytes 2359300
  68.3 192.4 %reduce-scatter.2.cloned.1.call-start = ((), (), s32[]{:S(2)}) async-start(), calls=%async_computation.4 | async-start | bytes 5898240 | tf_op jit(solution)/shard_map/reduce_scatter | solution.py:114
  68.4 11.8 %collective-permute-start = (bf16[2,1,48,256]{3,2,1,0:T(8,128)(2,1)S(1)}, bf16[2,1,48,256]{3,2,1,0:T(8,128)(2,1)S(1)}, u32[]{:S(2)}, u32[]{:S(2)}) collective-permute-start(bf16[2,1,48,256]{3,2,1,0:T(8,128)(2,1)S(1)} %get-tuple-element.13), channel_id=1, source_target_pairs={{0,1},{1,2},{2,3},{4,5},{5,6},{6,7},{8,9},{9,10},{10,11},{12,13},{... | collective-permute-start | bytes 147464 | tf_op jit(solution)/shard_map/ppermute | solution.py:14
  78.0 6.9 %collective-permute-start.1 = (bf16[2,1,48,256]{3,2,1,0:T(8,128)(2,1)S(1)}, bf16[2,1,48,256]{3,2,1,0:T(8,128)(2,1)S(1)}, u32[]{:S(2)}, u32[]{:S(2)}) collective-permute-start(bf16[2,1,48,256]{3,2,1,0:T(8,128)(2,1)S(1)} %get-tuple-element.14), channel_id=1, source_target_pairs={{1,0},{2,1},{3,2},{5,4},{6,5},{7,6},{9,8},{10,9},{11,10},{13,12},{... | collective-permute-start | bytes 147464 | tf_op jit(solution)/shard_map/ppermute | solution.py:17
  134.1 8.1 %copy-start.3 = (bf16[2,589824]{1,0:T(2,128)(2,1)}, bf16[2,589824]{1,0:T(2,128)(2,1)S(1)}, u32[]{:S(2)}) copy-start(bf16[2,589824]{1,0:T(2,128)(2,1)S(1)} %get-tuple-element.4) | copy-start | bytes 7077892
  134.1 13.0 %copy-start.4 = (bf16[2,589824]{1,0:T(2,128)(2,1)}, bf16[2,589824]{1,0:T(2,128)(2,1)S(1)}, u32[]{:S(2)}) copy-start(bf16[2,589824]{1,0:T(2,128)(2,1)S(1)} %get-tuple-element.3) | copy-start | bytes 7077892
  142.2 11.0 %collective-permute-start.2 = (bf16[2,1,48,256]{3,2,1,0:T(8,128)(2,1)S(1)}, bf16[2,1,48,256]{3,2,1,0:T(8,128)(2,1)S(1)}, u32[]{:S(2)}, u32[]{:S(2)}) collective-permute-start(bf16[2,1,48,256]{3,2,1,0:T(8,128)(2,1)S(1)} %get-tuple-element.11), channel_id=1, source_target_pairs={{0,1},{1,2},{2,3},{4,5},{5,6},{6,7},{8,9},{9,10},{10,11},{12,13},{... | collective-permute-start | bytes 147464 | tf_op jit(solution)/shard_map/ppermute | solution.py:14
  144.3 8.9 %collective-permute-start.3 = (bf16[2,1,48,256]{3,2,1,0:T(8,128)(2,1)S(1)}, bf16[2,1,48,256]{3,2,1,0:T(8,128)(2,1)S(1)}, u32[]{:S(2)}, u32[]{:S(2)}) collective-permute-start(bf16[2,1,48,256]{3,2,1,0:T(8,128)(2,1)S(1)} %get-tuple-element.12), channel_id=1, source_target_pairs={{1,0},{2,1},{3,2},{5,4},{6,5},{7,6},{9,8},{10,9},{11,10},{13,12},{... | collective-permute-start | bytes 147464 | tf_op jit(solution)/shard_map/ppermute | solution.py:17
  154.3 1.7 copy-start.5
  154.3 1.8 copy-start.9
  159.5 17.6 %collective-permute-start.4 = (bf16[2,1,48,256]{3,2,1,0:T(8,128)(2,1)S(1)}, bf16[2,1,48,256]{3,2,1,0:T(8,128)(2,1)S(1)}, u32[]{:S(2)}, u32[]{:S(2)}) collective-permute-start(bf16[2,1,48,256]{3,2,1,0:T(8,128)(2,1)S(1)} %get-tuple-element.9), channel_id=1, source_target_pairs={{0,1},{1,2},{2,3},{4,5},{5,6},{6,7},{8,9},{9,10},{10,11},{12,13},{... | collective-permute-start | bytes 147464 | tf_op jit(solution)/shard_map/ppermute | solution.py:14
  164.4 12.8 %collective-permute-start.5 = (bf16[2,1,48,256]{3,2,1,0:T(8,128)(2,1)S(1)}, bf16[2,1,48,256]{3,2,1,0:T(8,128)(2,1)S(1)}, u32[]{:S(2)}, u32[]{:S(2)}) collective-permute-start(bf16[2,1,48,256]{3,2,1,0:T(8,128)(2,1)S(1)} %get-tuple-element.10), channel_id=1, source_target_pairs={{1,0},{2,1},{3,2},{5,4},{6,5},{7,6},{9,8},{10,9},{11,10},{13,12},{... | collective-permute-start | bytes 147464 | tf_op jit(solution)/shard_map/ppermute | solution.py:17
  178.2 1.7 copy-start.7
  178.2 2.1 copy-start.10
  194.4 1.7 copy-start.6
  198.6 15.3 %collective-permute-start.6 = (bf16[2,1,48,256]{3,2,1,0:T(8,128)(2,1)S(1)}, bf16[2,1,48,256]{3,2,1,0:T(8,128)(2,1)S(1)}, u32[]{:S(2)}, u32[]{:S(2)}) collective-permute-start(bf16[2,1,48,256]{3,2,1,0:T(8,128)(2,1)S(1)} %get-tuple-element.7), channel_id=1, source_target_pairs={{0,1},{1,2},{2,3},{4,5},{5,6},{6,7},{8,9},{9,10},{10,11},{12,13},{... | collective-permute-start | bytes 147464 | tf_op jit(solution)/shard_map/ppermute | solution.py:14
  203.7 10.1 %collective-permute-start.7 = (bf16[2,1,48,256]{3,2,1,0:T(8,128)(2,1)S(1)}, bf16[2,1,48,256]{3,2,1,0:T(8,128)(2,1)S(1)}, u32[]{:S(2)}, u32[]{:S(2)}) collective-permute-start(bf16[2,1,48,256]{3,2,1,0:T(8,128)(2,1)S(1)} %get-tuple-element.8), channel_id=1, source_target_pairs={{1,0},{2,1},{3,2},{5,4},{6,5},{7,6},{9,8},{10,9},{11,10},{13,12},{... | collective-permute-start | bytes 147464 | tf_op jit(solution)/shard_map/ppermute | solution.py:17
  264.2 39.1 %all-to-all-start.2 = ((bf16[64,2,4608]{2,1,0:T(2,128)(2,1)}), bf16[64,2,4608]{2,1,0:T(2,128)(2,1)S(1)}, u32[]{:S(2)}, u32[]{:S(2)}) async-start(bf16[64,2,4608]{2,1,0:T(2,128)(2,1)} %copy.32), calls=%async_computation.3 | async-start | bytes 2359296 | tf_op jit(solution)/shard_map/all_to_all | solution.py:117
  275.8 6.6 %copy-start.8 = (bf16[2,3,3,256,256]{3,4,2,1,0:T(8,128)(2,1)S(1)}, bf16[2,3,3,256,256]{3,4,2,1,0:T(8,128)(2,1)}, u32[]{:S(2)}) copy-start(bf16[2,3,3,256,256]{3,4,2,1,0:T(8,128)(2,1)} %rev.7) | copy-start | bytes 7077892
  282.5 24.5 %copy-start.1 = (bf16[256,512]{1,0:T(8,128)(2,1)S(1)}, bf16[256,512]{1,0:T(8,128)(2,1)}, u32[]{:S(2)}) copy-start(bf16[256,512]{1,0:T(8,128)(2,1)} %param.8) | copy-start | bytes 786436
Sparse Core Ops, SparseCore 0:
  68.4 45.6 all-gather.2
  198.7 62.0 reduce-scatter.1

commit v2 on v0

v2 whole, which is shorter than its diff:
```python
import functools
import math

import jax
import jax.numpy as jnp
from jax import lax
from jax.experimental import pallas as pl
from jax.experimental.pallas import tpu as pltpu
from jax.sharding import PartitionSpec as P

MESH = pl.DeviceIdType.MESH
LANES = 128
GROUP = 16


def smooth_act(values):
    return values * jax.nn.sigmoid(values)


def smooth_slope(values):
    sig = jax.nn.sigmoid(values)
    return sig * (1.0 + values * (1.0 - sig))


def light_codes(light_ids, tile_offsets, light_table):
    halfway = light_table.shape[1] // 2
    onehot = (
        light_ids[:, None] == jnp.arange(light_table.shape[0], dtype=jnp.int32)[None, :]
    ).astype(jnp.bfloat16)
    looked = jnp.dot(onehot, light_table, preferred_element_type=jnp.float32)
    rates = jnp.exp(-math.log(1000.0) * jnp.arange(halfway, dtype=jnp.float32) / halfway)
    angles = tile_offsets.astype(jnp.float32)[:, None] * rates[None, :]
    summed = looked + jnp.concatenate([jnp.sin(angles), jnp.cos(angles)], axis=1)
    return (summed * lax.rsqrt(jnp.mean(summed * summed, axis=1, keepdims=True) + 1e-06)).astype(
        jnp.bfloat16
    )


def place():
    light, tex = lax.axis_index("light"), lax.axis_index("tex")
    half, core = tex // 2, tex % 2
    return light, half, core, light * 2 + half


def peer(chip, core):
    return (chip // 2, (chip % 2) * 2 + core)


def await_bytes(ref, sem):
    pltpu.make_async_copy(ref, ref, sem).wait()


def swap_copies(src, dst, halo, send, recv, start):
    light, half, core, _ = place()
    rows = src.shape[1]

    def go(source, target, to_half, to_core, slot, number):
        here = jnp.logical_and(to_half == half, to_core == core)

        @pl.when(here)
        def _():
            if start:
                pltpu.make_async_copy(source, target, recv.at[slot]).start()

        @pl.when(jnp.logical_not(here))
        def _():
            copy = pltpu.make_async_remote_copy(
                src_ref=source,
                dst_ref=target,
                send_sem=send.at[number],
                recv_sem=recv.at[slot],
                device_id=(light, to_half * 2 + to_core),
                device_id_type=MESH,
            )
            if start:
                copy.start()
            else:
                copy.wait_send()

    for to_half in range(2):
        for own in range(2):

            @pl.when(core == own)
            def _():
                go(
                    src.at[to_half],
                    dst.at[pl.ds(own * rows + halo, rows)],
                    to_half,
                    half,
                    own,
                    to_half,
                )

        @pl.when(jnp.logical_and(half == 1, core == 0))
        def _():
            go(
                src.at[to_half, pl.ds(0, halo)],
                dst.at[pl.ds(2 * rows + halo, halo)],
                to_half,
                0,
                2,
                2 + to_half,
            )

        @pl.when(jnp.logical_and(half == 0, core == 1))
        def _():
            go(
                src.at[to_half, pl.ds(rows - halo, halo)],
                dst.at[pl.ds(0, halo)],
                to_half,
                1,
                2,
                2 + to_half,
            )


def swap_arrivals(src, dst, halo, recv):
    rows = src.shape[1]
    for slot, count in ((0, rows), (1, rows), (2, halo)):
        await_bytes(dst.at[pl.ds(0, count)], recv.at[slot])


def forward_kernel(
    scale,
    lights,
    codes_ref,
    hyper_ref,
    feat_ref,
    up_ref,
    blocks_ref,
    codes_out,
    feat_out,
    up_out,
    hyper,
    codes,
    wide,
    ready,
    hyper_sem,
    code_send,
    code_recv,
    own_sem,
    block_send,
    block_recv,
    pass_send,
    pass_recv,
    feat_send,
    feat_recv,
    up_send,
    up_recv,
):
    light, half, core, me = place()
    chips = 2 * lights
    groups = chips // GROUP
    load = pltpu.make_async_copy(hyper_ref, hyper, hyper_sem)
    load.start()

    codes[pl.ds(pl.multiple_of(light * 8, 8), 8), :] = codes_ref[...]

    def send_codes(step, _):
        other = lax.rem(light + step, lights)
        pltpu.make_async_remote_copy(
            src_ref=codes_ref,
            dst_ref=codes.at[pl.ds(pl.multiple_of(light * 8, 8), 8)],
            send_sem=code_send,
            recv_sem=code_recv,
            device_id=(other, half * 2 + core),
            device_id_type=MESH,
        ).start()
        return 0

    lax.fori_loop(1, lights, send_codes, 0)
    swap_copies(feat_ref, feat_out, 4, feat_send, feat_recv, True)
    swap_copies(up_ref, up_out, 2, up_send, up_recv, True)
    arrived = codes.at[pl.ds(0, 8 * (lights - 1))]
    await_bytes(arrived, code_recv)
    parts = [codes[pl.ds(k, chips, stride=4), :] for k in range(4)]
    table = jnp.concatenate(parts, axis=1).astype(jnp.bfloat16)
    codes_out[...] = table
    load.wait()
    rows = hyper.shape[1] // (2 * LANES)
    for row in range(rows):
        product = scale * jnp.dot(
            table,
            hyper[:, row * 2 * LANES : (row + 1) * 2 * LANES],
            preferred_element_type=jnp.float32,
        )
        wide[pl.ds(row, chips, stride=40), :] = product[:, :LANES]
        wide[pl.ds(rows + row, chips, stride=40), :] = product[:, LANES:]

    def narrow(chip, _):
        ready[chip] = wide[pl.ds(pl.multiple_of(chip * 40, 8), 2 * rows), :].astype(jnp.bfloat16)
        return 0

    lax.fori_loop(0, chips, narrow, 0)

    keep = pltpu.make_async_copy(ready.at[me], blocks_ref.at[core, me], own_sem)
    keep.start()
    my_group, my_slot = me // GROUP, me % GROUP

    def send_block(step, _):
        group = lax.rem(my_group + step // GROUP, groups)
        slot = lax.rem(my_slot + step % GROUP, GROUP)
        other = group * GROUP + slot
        pltpu.make_async_remote_copy(
            src_ref=ready.at[other],
            dst_ref=blocks_ref.at[core, me],
            send_sem=block_send,
            recv_sem=block_recv.at[my_group],
            device_id=peer(other, core),
            device_id_type=MESH,
        ).start()
        return 0

    lax.fori_loop(1, chips, send_block, 0)

    def to_sibling(group):
        span = blocks_ref.at[core, pl.ds(group * GROUP, GROUP)]
        return pltpu.make_async_remote_copy(
            src_ref=span,
            dst_ref=span,
            send_sem=pass_send.at[group],
            recv_sem=pass_recv.at[group],
            device_id=(light, half * 2 + 1 - core),
            device_id_type=MESH,
        )

    keep.wait()
    await_bytes(blocks_ref.at[core, pl.ds(0, GROUP - 1)], block_recv.at[my_group])
    to_sibling(my_group).start()

    def pass_on(step, _):
        group = lax.rem(my_group + groups - step, groups)
        await_bytes(blocks_ref.at[core, pl.ds(0, GROUP)], block_recv.at[group])
        to_sibling(group).start()
        return 0

    lax.fori_loop(1, groups, pass_on, 0)

    def finish(group, _):
        to_sibling(group).wait()
        return 0

    lax.fori_loop(0, groups, finish, 0)
    await_bytes(ready.at[pl.ds(0, chips - 1)], block_send)
    await_bytes(arrived, code_send)
    swap_copies(feat_ref, feat_out, 4, feat_send, feat_recv, False)
    swap_copies(up_ref, up_out, 2, up_send, up_recv, False)
    swap_arrivals(feat_ref, feat_out, 4, feat_recv)
    swap_arrivals(up_ref, up_out, 2, up_recv)


def forward_exchange(scale, lights, codes, hyper_weight, features, upstream):
    chips = 2 * lights
    depth, own_len = hyper_weight.shape
    block_rows = own_len // LANES
    _, rows, columns, channels = features.shape
    dma = pltpu.SemaphoreType.DMA
    anywhere = pl.BlockSpec(memory_space=pl.ANY)
    vmem = pl.BlockSpec(memory_space=pltpu.VMEM)
    return pl.pallas_call(
        functools.partial(forward_kernel, scale, lights),
        out_shape=(
            jax.ShapeDtypeStruct((2, chips, block_rows, LANES), jnp.bfloat16),
            jax.ShapeDtypeStruct((chips, depth), jnp.bfloat16),
            jax.ShapeDtypeStruct((2 * rows + 8, columns, channels), jnp.bfloat16),
            jax.ShapeDtypeStruct((2 * rows + 4, columns, channels), jnp.bfloat16),
        ),
        in_specs=[vmem, anywhere, anywhere, anywhere],
        out_specs=(anywhere, vmem, anywhere, anywhere),
        scratch_shapes=[
            pltpu.VMEM((depth, own_len), jnp.bfloat16),
            pltpu.VMEM((8 * lights, LANES), jnp.float32),
            pltpu.VMEM((chips * 40, LANES), jnp.float32),
            pltpu.VMEM((chips, block_rows, LANES), jnp.bfloat16),
            dma,
            dma,
            dma,
            dma,
            dma,
            dma((chips // GROUP,)),
            dma((chips // GROUP,)),
            dma((chips // GROUP,)),
            dma((4,)),
            dma((3,)),
            dma((4,)),
            dma((3,)),
        ],
        compiler_params=pltpu.CompilerParams(
            has_side_effects=True, vmem_limit_bytes=40 * 1024 * 1024
        ),
    )(codes, hyper_weight, features, upstream)


def give_back(src, dst, send, recv, start):
    light, half, core, _ = place()
    rows = dst.shape[1]
    for piece in range(2):
        here = jnp.logical_and(core == half, piece == core)
        source = src.at[pl.ds(piece * rows, rows)]
        for own in range(2):

            @pl.when(jnp.logical_and(here, half == own))
            def _():
                if start:
                    pltpu.make_async_copy(source, dst.at[own], recv.at[own]).start()

            @pl.when(jnp.logical_and(jnp.logical_not(here), half == own))
            def _():
                copy = pltpu.make_async_remote_copy(
                    src_ref=source,
                    dst_ref=dst.at[own],
                    send_sem=send.at[piece],
                    recv_sem=recv.at[own],
                    device_id=(light, core * 2 + piece),
                    device_id_type=MESH,
                )
                if start:
                    copy.start()
                else:
                    copy.wait_send()


def backward_kernel(
    lights,
    parts_ref,
    relit_ref,
    grad_ref,
    sums_ref,
    relit_out,
    grad_out,
    mine,
    theirs,
    ready,
    mine_sem,
    core_send,
    core_recv,
    own_sem,
    block_send,
    block_recv,
    relit_send,
    relit_recv,
    grad_send,
    grad_recv,
):
    light, half, core, me = place()
    chips = 2 * lights
    groups = chips // GROUP
    my_group, my_slot = me // GROUP, me % GROUP
    load = pltpu.make_async_copy(parts_ref.at[core], mine, mine_sem)
    load.start()

    def to_sibling(group):
        return pltpu.make_async_remote_copy(
            src_ref=parts_ref.at[1 - core, pl.ds(group * GROUP, GROUP)],
            dst_ref=theirs.at[pl.ds(group * GROUP, GROUP)],
            send_sem=core_send.at[group],
            recv_sem=core_recv.at[group],
            device_id=(light, half * 2 + 1 - core),
            device_id_type=MESH,
        )

    def start_group(step, _):
        to_sibling(lax.rem(my_group + step, groups)).start()
        return 0

    lax.fori_loop(0, groups, start_group, 0)
    give_back(relit_ref, relit_out, relit_send, relit_recv, True)
    give_back(grad_ref, grad_out, grad_send, grad_recv, True)
    load.wait()

    def send_block(other):
        pltpu.make_async_remote_copy(
            src_ref=ready.at[other],
            dst_ref=sums_ref.at[me],
            send_sem=block_send,
            recv_sem=block_recv,
            device_id=peer(other, core),
            device_id_type=MESH,
        ).start()

    def do_group(step, _):
        group = lax.rem(my_group + step, groups)
        to_sibling(group).wait_recv()

        def do_block(slot, _):
            other = group * GROUP + lax.rem(my_slot + slot, GROUP)
            ready[other] = (
                mine[other].astype(jnp.float32) + theirs[other].astype(jnp.float32)
            ).astype(jnp.bfloat16)

            @pl.when(other != me)
            def _():
                send_block(other)

            return 0

        return lax.fori_loop(0, GROUP, do_block, 0)

    lax.fori_loop(0, groups, do_group, 0)
    keep = pltpu.make_async_copy(ready.at[me], sums_ref.at[me], own_sem)
    keep.start()
    keep.wait()

    def finish(group, _):
        to_sibling(group).wait_send()
        return 0

    lax.fori_loop(0, groups, finish, 0)
    give_back(relit_ref, relit_out, relit_send, relit_recv, False)
    give_back(grad_ref, grad_out, grad_send, grad_recv, False)
    for own in range(2):
        await_bytes(relit_out.at[own], relit_recv.at[own])
        await_bytes(grad_out.at[own], grad_recv.at[own])
    await_bytes(ready.at[pl.ds(0, chips - 1)], block_send)
    await_bytes(sums_ref.at[pl.ds(0, chips - 1)], block_recv)


def backward_exchange(lights, parts, relit, feature_grad):
    _, chips, block_rows, lanes = parts.shape
    rows, columns, channels = relit.shape
    dma = pltpu.SemaphoreType.DMA
    anywhere = pl.BlockSpec(memory_space=pl.ANY)
    image = jax.ShapeDtypeStruct((2, rows // 2, columns, channels), jnp.bfloat16)
    return pl.pallas_call(
        functools.partial(backward_kernel, lights),
        out_shape=(
            jax.ShapeDtypeStruct((chips, block_rows, lanes), jnp.bfloat16),
            image,
            image,
        ),
        in_specs=[anywhere] * 3,
        out_specs=(anywhere,) * 3,
        scratch_shapes=[
            pltpu.VMEM((chips, block_rows, lanes), jnp.bfloat16),
            pltpu.VMEM((chips, block_rows, lanes), jnp.bfloat16),
            pltpu.VMEM((chips, block_rows, lanes), jnp.bfloat16),
            dma,
            dma((chips // GROUP,)),
            dma((chips // GROUP,)),
            dma,
            dma,
            dma,
            dma((2,)),
            dma((2,)),
            dma((2,)),
            dma((2,)),
        ],
        compiler_params=pltpu.CompilerParams(
            has_side_effects=True, vmem_limit_bytes=40 * 1024 * 1024
        ),
    )(parts, relit, feature_grad)


def conv(image, kernel):
    return lax.conv_general_dilated(
        image[None],
        kernel,
        (1, 1),
        ((0, 0), (1, 1)),
        dimension_numbers=("NHWC", "HWIO", "NHWC"),
        preferred_element_type=jnp.float32,
    )[0]


def conv_back(image, kernel):
    return lax.conv_general_dilated(
        image[None],
        kernel[::-1, ::-1],
        (1, 1),
        ((0, 0), (1, 1)),
        dimension_numbers=("NHWC", "HWOI", "NHWC"),
        preferred_element_type=jnp.float32,
    )[0]


def kernel_grad(image, upstream):
    return lax.conv_general_dilated(
        image[None],
        upstream[None],
        (1, 1),
        ((0, 0), (1, 1)),
        dimension_numbers=("CHWN", "IHWO", "HWNC"),
        preferred_element_type=jnp.float32,
    )


def shards(light_ids, tile_offsets, light_table, hyper_weight, features, upstream_grad):
    rows_dev, channels = features.shape[1], features.shape[3]
    scale = 1.0 / math.sqrt(9 * channels)
    lights = lax.axis_size("light")
    rows = 2 * rows_dev
    core = lax.axis_index("tex") % 2
    own_codes = light_codes(light_ids, tile_offsets, light_table)
    blocks, codes, feats, upstream = forward_exchange(
        scale,
        lights,
        own_codes.astype(jnp.float32).reshape(8, LANES),
        hyper_weight,
        features,
        upstream_grad,
    )
    chips = 2 * lights
    taps = hyper_weight.shape[1] // channels
    kernels = (
        blocks.reshape(2, chips, 2, taps, LANES)
        .transpose(1, 0, 3, 2, 4)
        .reshape(2, 3, 3, channels, channels)
    )

    def inside(values, halo):
        spot = jnp.arange(rows + 2 * halo) + core * rows - halo
        kept = jnp.logical_and(spot >= 0, spot < 2 * rows)[:, None, None]
        return jnp.where(kept, values, jnp.zeros_like(values))

    feats = inside(feats, 4)
    first_pre = conv(feats, kernels[0])
    hidden = inside(smooth_act(first_pre), 3).astype(jnp.bfloat16)
    second_pre = conv(hidden, kernels[1])
    relit = smooth_act(second_pre[2 : rows + 2]).astype(jnp.bfloat16)
    second_grad = inside(upstream * smooth_slope(second_pre), 2).astype(jnp.bfloat16)
    hidden_grad = conv_back(second_grad, kernels[1])
    first_grad = inside(hidden_grad * smooth_slope(first_pre[2 : rows + 4]), 1).astype(
        jnp.bfloat16
    )
    feature_grad = conv_back(first_grad, kernels[0]).astype(jnp.bfloat16)
    first_kgrad = kernel_grad(feats[3 : rows + 5], first_grad[1 : rows + 1])
    second_kgrad = kernel_grad(hidden[2 : rows + 4], second_grad[2 : rows + 2])
    parts = (
        jnp.stack([first_kgrad, second_kgrad])
        .astype(jnp.bfloat16)
        .reshape(chips, 2, taps, 2, LANES)
        .transpose(1, 0, 3, 2, 4)
        .reshape(2, chips, 2 * taps, LANES)
    )
    sums, relit, feature_grad = backward_exchange(lights, parts, relit, feature_grad)
    summed = (
        sums.reshape(chips, 2, taps, LANES).transpose(0, 2, 1, 3).reshape(chips, taps * channels)
    )
    hyper_grad = (
        scale * jnp.einsum("lz,ls->zs", codes, summed, preferred_element_type=jnp.float32)
    ).astype(jnp.bfloat16)
    return (relit, feature_grad, hyper_grad)


def solution(mesh):
    in_specs = (
        P("light"),
        P("light"),
        P(),
        P(None, ("light", "tex")),
        P("light", "tex", None, None),
        P("light", "tex", None, None),
    )
    out_specs = (
        P("light", "tex", None, None),
        P("light", "tex", None, None),
        P(None, ("light", "tex")),
    )
    return jax.shard_map(shards, mesh=mesh, in_specs=in_specs, out_specs=out_specs, check_vma=False)
```

time: 615 us -> 242 us (0.39)
  the two profiles are of different devices: /device:TPU:1 before, /device:TPU:8 now
where the time goes in v2:
time: 242 us; the launch traced here: 238 us
  Pallas kernels  109 us (45%)
  matrix products  82.1 us (34%)
  local copies, waits for them, and re-layouts  39.3 us (16%)
  other arithmetic  6.51 us (3%)
    pallas_call x1, Pallas kernels, forward_exchange(): pl.pallas_call(functools.partial(forward_kernel, scale, lights), out_shap...  60.8 us
    pallas_call x1, Pallas kernels, backward_exchange(): pl.pallas_call(functools.partial(backward_kernel, lights), out_shape=(jax...  47.9 us
    conv_general_dilated x2, matrix products, conv(): lax.conv_general_dilated(image[None], kernel, (1, 1), ((0, 0), (1, 1)), d...  27.8 us
    conv_general_dilated x2, matrix products, conv_back(): lax.conv_general_dilated(image[None], kernel[::-1, ::-1], (1, 1), ((0, 0)...  27.1 us
    conv_general_dilated x2, matrix products, kernel_grad(): lax.conv_general_dilated(image[None], upstream[None], (1, 1), ((0, 0), (1...  21.4 us
    unnamed x36, local copies, waits for them, and re-layouts  9.66 us
    convert_element_type x2, local copies, waits for them, and re-layouts, shards(): parts = jnp.stack([first_kgrad, second_kgrad]).astype(jnp.bfloat16).resha...  7.95 us
    dot_general x1, matrix products, shards(): jnp.einsum('lz,ls->zs', codes, summed, preferred_element_type=jnp.float32)  4.92 us

profile of v2, /device:TPU:8, one launch (start us, length us, event | category | flops | bytes accessed | tf_op | source)
XLA Modules:
  0.0 237.8 jit_solution(9413872487693935889)
XLA Ops:
  0.7 0.6 slice.52
  1.4 0.6 slice.55
  1.9 0.7 convert_element_type.42
  2.7 1.0 multiply_reduce_fusion
  3.8 2.3 copy-done.2
  6.1 1.1 copy-done.3
  7.3 1.1 copy-done.4
  8.4 60.8 %shard_map.85 = (bf16[2,128,36,128]{3,2,1,0:T(8,128)(2,1)S(1)}, bf16[128,512]{1,0:T(8,128)(2,1)S(1)}, bf16[40,48,256]{2,1,0:T(8,128)(2,1)S(1)}, bf16[36,48,256]{2,1,0:T(8,128)(2,1)S(1)}) custom-call(f32[8,128]{1,0:T(8,128)S(1)} %reshape.88.codes_ref, bf16[512,4608]{1,0:T(8,128)(2,1)S(1)} %copy-done.2, bf16[2,16,48,256]{3,2,1,0:T(8,128)(2,1)S(1)} %copy-done.3, ...), custom_call_target="tpu_custom_call" | custom-call | tf_op jit(solution)/shard_map/pallas_call | solution.py:260
  69.2 1.1 fusion.76
  70.3 0.1 broadcast_select_fusion.2
  70.4 1.0 slice_bitcast_fusion
  71.4 0.6 copy.20
  72.0 1.5 fusion.68
  73.5 1.2 copy.21
  74.7 2.0 squeeze.18
  76.8 13.2 %fusion = f32[1,38,48,256]{3,0,2,1:T(1,128)S(1)} fusion(bf16[3,3,256,256]{3,2,1,0:T(8,128)(2,1)} %squeeze.18, bf16[1,40,48,256]{3,2,1,0:T(8,128)(2,1)} %fusion.76), kind=kOutput, calls=%fused_computation.4 | convolution fusion | flops 2121793536 | bytes 4030464 | tf_op jit(solution)/shard_map/conv_general_dilated | solution.py:455
  90.0 2.4 %copy.23 = bf16[64,2,18,2,128]{4,3,2,1,0:T(2,128)(2,1)} copy(bf16[64,2,18,2,128]{4,0,2,3,1:T(8,128)(2,1)S(1)} %copy-done.8) | data formatting | bytes 2359296 | tf_op jit(solution)/shard_map/slice | solution.py:518
  92.5 3.9 %squeeze.19 = bf16[3,3,256,256]{3,2,1,0:T(8,128)(2,1)} reshape(bf16[64,2,18,2,128]{4,3,2,1,0:T(2,128)(2,1)} %copy.23) | data formatting | bytes 2359296 | tf_op jit(solution)/shard_map/squeeze | solution.py:518
  96.3 2.4 slice.47
  98.7 14.6 %fusion.3 = f32[1,36,48,256]{3,0,2,1:T(1,128)S(1)} fusion(bf16[3,3,256,256]{3,2,1,0:T(8,128)(2,1)S(1)} %copy-done.10, f32[1,38,48,256]{3,0,2,1:T(1,128)S(1)} %fusion, pred[38]{0:T(512)(128)(4,1)S(1)} %compare_and_fusion), kind=kOutput, calls=%fused_computation.9 | convolution fusion | flops 2012921856 | bytes 4816934 | tf_op jit(solution)/shard_map/conv_general_dilated | solution.py:455
  113.3 0.8 fusion.12
  114.1 1.1 slice.57
  115.2 0.4 multiply_convert_fusion.1.relit_ref
  115.6 10.6 %fusion.13 = f32[1,34,48,256]{3,0,2,1:T(1,128)S(1)} fusion(bf16[3,3,256,256]{3,2,1,0:T(8,128)(2,1)S(1)} %copy-done.10, bf16[1,36,48,256]{3,2,1,0:T(8,128)(2,1)S(1)} %bitcast.81), kind=kOutput, calls=%fused_computation.20 | convolution fusion | flops 1898446848 | bytes 3735552 | tf_op jit(solution)/shard_map/conv_general_dilated | solution.py:466
  126.2 16.5 %fusion.24 = bf16[1,32,48,256]{3,0,2,1:T(2,128)(2,1)S(1)} fusion(bf16[3,3,256,256]{3,2,1,0:T(8,128)(2,1)S(1)} %copy-done.9, f32[1,34,48,256]{3,0,2,1:T(1,128)S(1)} %fusion.13, pred[34]{0:T(512)(128)(4,1)S(1)} %compare_and_fusion.2, f32[1,38,48,256]{3,0,2,1:T(1,128)S(1)} %fusion), kind=kOutput, calls=%fused_computation.36 | convolution fusion | flops 1790951424 | bytes 5308928 | tf_op jit(solution)/shard_map/conv_general_dilated | solution.py:466
  142.7 0.1 copy.85
  142.9 0.9 slice_bitcast_fusion.1
  143.8 0.6 copy-done.7
  144.5 0.4 copy_bitcast_fusion.1
  144.9 0.6 add_divide_fusion
  145.6 0.3 fusion.57
  145.9 0.8 copy-done.12
  146.7 11.1 %fusion.46 = bf16[1,3,3,256,256]{4,3,2,1,0:T(8,128)(2,1)} fusion(bf16[1,32,48,256]{3,2,1,0:T(8,128)(2,1)S(1)} %fusion.57, bf16[1,34,48,256]{3,2,1,0:T(8,128)(2,1)S(1)} %copy-done.12), kind=kOutput, calls=%fused_computation.51 | convolution fusion | flops 1787363328 | bytes 2801664 | tf_op jit(solution)/shard_map/conv_general_dilated | solution.py:477
  157.8 0.2 fusion.66
  158.1 0.5 copy-done.14
  158.7 0.5 fusion.55
  159.1 0.6 copy-done.13
  159.8 10.3 %fusion.41 = bf16[1,3,3,256,256]{4,3,2,1,0:T(8,128)(2,1)S(1)} fusion(bf16[1,32,48,256]{3,2,1,0:T(8,128)(2,1)S(1)} %copy-done.13, bf16[1,34,48,256]{3,2,1,0:T(8,128)(2,1)S(1)} %fusion.55), kind=kOutput, calls=%fused_computation.50 | convolution fusion | flops 1787363328 | bytes 2801664 | tf_op jit(solution)/shard_map/conv_general_dilated | solution.py:477
  170.1 1.6 pad_maximum_fusion
  171.7 5.7 %convert_element_type.49 = bf16[128,2,18,2,128]{4,3,2,1,0:T(2,128)(2,1)} reshape(bf16[2,3,3,256,256]{4,3,2,1,0:T(8,128)(2,1)} %pad_maximum_fusion) | data formatting | bytes 4718592 | tf_op jit(solution)/shard_map/convert_element_type | solution.py:530
  177.4 2.2 copy.29
  179.6 1.6 copy.32.parts_ref
  181.2 47.9 %shard_map.86 = (bf16[128,36,128]{2,1,0:T(8,128)(2,1)S(1)}, bf16[2,16,48,256]{3,2,1,0:T(8,128)(2,1)S(1)}, bf16[2,16,48,256]{3,2,1,0:T(8,128)(2,1)S(1)}) custom-call(bf16[2,128,36,128]{3,2,1,0:T(8,128)(2,1)S(1)} %copy.32.parts_ref, bf16[32,48,256]{2,1,0:T(8,128)(2,1)S(1)} %multiply_convert_fusion.1.relit_ref, bf16[32,48,256]{2,1,0:T(8,128)(2,1)S(1)} %bitcast.75), custom_call_target="tpu_custom_call" | custom-call | tf_op jit(solution)/shard_map/pallas_call | solution.py:424
  229.1 0.3 copy.33
  229.4 1.4 copy.34
  230.9 4.9 %multiply_convert_fusion = bf16[512,4608]{1,0:T(8,128)(2,1)} fusion(bf16[128,512]{1,0:T(8,128)(2,1)S(1)} %get-tuple-element.15, bf16[128,4608]{0,1:T(8,128)(2,1)} %bitcast.80), kind=kOutput, calls=%fused_computation | convolution fusion | flops 608698368 | bytes 6029312 | tf_op jit(solution)/shard_map/lz,ls->zs/dot_general | solution.py:540
  235.8 0.9 copy.88
  236.7 0.9 copy.89
  (35 shorter events, 0.5 us)
Async XLA Ops:
  0.6 2.1 copy-start
  3.8 2.3 copy-start.2
  6.1 1.1 copy-start.3
  7.3 1.1 copy-start.4
  76.8 13.2 %copy-start.8 = (bf16[64,2,18,2,128]{4,0,2,3,1:T(8,128)(2,1)S(1)}, bf16[64,2,18,2,128]{4,0,2,3,1:T(8,128)(2,1)}, u32[]{:S(2)}) copy-start(bf16[64,2,18,2,128]{4,0,2,3,1:T(8,128)(2,1)} %get-tuple-element.18) | copy-start | bytes 3538948
  90.0 36.2 %copy-start.5 = (f32[1,38,48,256]{3,0,2,1:T(1,128)}, f32[1,38,48,256]{3,0,2,1:T(1,128)S(1)}, u32[]{:S(2)}) copy-start(f32[1,38,48,256]{3,0,2,1:T(1,128)S(1)} %fusion) | copy-start | bytes 5603332
  96.3 2.4 copy-start.10
  115.6 10.6 %copy-start.9 = (bf16[3,3,256,256]{3,2,1,0:T(8,128)(2,1)S(1)}, bf16[3,3,256,256]{3,2,1,0:T(8,128)(2,1)}, u32[]{:S(2)}) copy-start(bf16[3,3,256,256]{3,2,1,0:T(8,128)(2,1)} %squeeze.18) | copy-start | bytes 3538948
  142.7 1.7 copy-start.7
  144.9 0.7 copy-start.15
  145.5 1.1 copy-start.12
  146.7 11.1 %copy-start.6 = (f32[1,38,48,256]{3,0,2,1:T(1,128)S(1)}, f32[1,38,48,256]{3,0,2,1:T(1,128)}, u32[]{:S(2)}) copy-start(f32[1,38,48,256]{3,0,2,1:T(1,128)} %copy-done.5) | copy-start | bytes 5603332
  158.0 0.7 copy-start.14
  158.7 1.1 copy-start.13
  159.8 10.3 %copy-start.11 = (bf16[1,3,3,256,256]{4,3,2,1,0:T(8,128)(2,1)S(1)}, bf16[1,3,3,256,256]{4,3,2,1,0:T(8,128)(2,1)}, u32[]{:S(2)}) copy-start(bf16[1,3,3,256,256]{4,3,2,1,0:T(8,128)(2,1)} %fusion.46) | copy-start | bytes 3538948
  230.9 6.7 %copy-start.1 = (bf16[256,512]{1,0:T(8,128)(2,1)S(1)}, bf16[256,512]{1,0:T(8,128)(2,1)}, u32[]{:S(2)}) copy-start(bf16[256,512]{1,0:T(8,128)(2,1)} %param.8) | copy-start | bytes 786436

commit v3 on v2

--- a/solution.py
+++ b/solution.py
@@ -11,15 +11,8 @@
 MESH = pl.DeviceIdType.MESH
 LANES = 128
 GROUP = 16
-
-
-def smooth_act(values):
-    return values * jax.nn.sigmoid(values)
-
-
-def smooth_slope(values):
-    sig = jax.nn.sigmoid(values)
-    return sig * (1.0 + values * (1.0 - sig))
+HALO = 4
+VMEM = 60 * 1024 * 1024
 
 
 def light_codes(light_ids, tile_offsets, light_table):
@@ -46,13 +39,32 @@
     return (chip // 2, (chip % 2) * 2 + core)
 
 
+def greet():
+    light, half, core, me = place()
+    chips = 2 * lax.axis_size("light")
+    barrier = pltpu.get_barrier_semaphore()
+
+    def signal(target):
+        pl.semaphore_signal(barrier, inc=1, device_id=target, device_id_type=MESH)
+
+    def signal_chip(step, _):
+        signal(peer(lax.rem(me + step, chips), core))
+        return 0
+
+    lax.fori_loop(1, chips, signal_chip, 0)
+    signal((light, half * 2 + 1 - core))
+    signal((light, (1 - half) * 2 + 1 - core))
+    pl.semaphore_wait(barrier, chips + 1)
+
+
 def await_bytes(ref, sem):
     pltpu.make_async_copy(ref, ref, sem).wait()
 
 
-def swap_copies(src, dst, halo, send, recv, start):
+def swap_copies(src, dst, send, recv, start):
     light, half, core, _ = place()
     rows = src.shape[1]
+    halo = dst.shape[0] - 2 * rows
 
     def go(source, target, to_half, to_core, slot, number):
         here = jnp.logical_and(to_half == half, to_core == core)
@@ -84,7 +96,7 @@
             def _():
                 go(
                     src.at[to_half],
-                    dst.at[pl.ds(own * rows + halo, rows)],
+                    dst.at[pl.ds(own * rows + halo * half, rows)],
                     to_half,
                     half,
                     own,
@@ -95,7 +107,7 @@
         def _():
             go(
                 src.at[to_half, pl.ds(0, halo)],
-                dst.at[pl.ds(2 * rows + halo, halo)],
+                dst.at[pl.ds(2 * rows, halo)],
                 to_half,
                 0,
                 2,
@@ -114,8 +126,9 @@
             )
 
 
-def swap_arrivals(src, dst, halo, recv):
+def swap_arrivals(src, dst, recv):
     rows = src.shape[1]
+    halo = dst.shape[0] - 2 * rows
     for slot, count in ((0, rows), (1, rows), (2, halo)):
         await_bytes(dst.at[pl.ds(0, count)], recv.at[slot])
 
@@ -153,6 +166,7 @@
     groups = chips // GROUP
     load = pltpu.make_async_copy(hyper_ref, hyper, hyper_sem)
     load.start()
+    greet()
 
     codes[pl.ds(pl.multiple_of(light * 8, 8), 8), :] = codes_ref[...]
 
@@ -169,8 +183,8 @@
         return 0
 
     lax.fori_loop(1, lights, send_codes, 0)
-    swap_copies(feat_ref, feat_out, 4, feat_send, feat_recv, True)
-    swap_copies(up_ref, up_out, 2, up_send, up_recv, True)
+    swap_copies(feat_ref, feat_out, feat_send, feat_recv, True)
+    swap_copies(up_ref, up_out, up_send, up_recv, True)
     arrived = codes.at[pl.ds(0, 8 * (lights - 1))]
     await_bytes(arrived, code_recv)
     parts = [codes[pl.ds(k, chips, stride=4), :] for k in range(4)]
@@ -187,12 +201,10 @@
         wide[pl.ds(row, chips, stride=40), :] = product[:, :LANES]
         wide[pl.ds(rows + row, chips, stride=40), :] = product[:, LANES:]
 
-    def narrow(chip, _):
+    def narrow(chip):
         ready[chip] = wide[pl.ds(pl.multiple_of(chip * 40, 8), 2 * rows), :].astype(jnp.bfloat16)
-        return 0
-
-    lax.fori_loop(0, chips, narrow, 0)
-
+
+    narrow(me)
     keep = pltpu.make_async_copy(ready.at[me], blocks_ref.at[core, me], own_sem)
     keep.start()
     my_group, my_slot = me // GROUP, me % GROUP
@@ -201,6 +213,7 @@
         group = lax.rem(my_group + step // GROUP, groups)
         slot = lax.rem(my_slot + step % GROUP, GROUP)
         other = group * GROUP + slot
+        narrow(other)
         pltpu.make_async_remote_copy(
             src_ref=ready.at[other],
             dst_ref=blocks_ref.at[core, me],
@@ -243,10 +256,10 @@
     lax.fori_loop(0, groups, finish, 0)
     await_bytes(ready.at[pl.ds(0, chips - 1)], block_send)
     await_bytes(arrived, code_send)
-    swap_copies(feat_ref, feat_out, 4, feat_send, feat_recv, False)
-    swap_copies(up_ref, up_out, 2, up_send, up_recv, False)
-    swap_arrivals(feat_ref, feat_out, 4, feat_recv)
-    swap_arrivals(up_ref, up_out, 2, up_recv)
+    swap_copies(feat_ref, feat_out, feat_send, feat_recv, False)
+    swap_copies(up_ref, up_out, up_send, up_recv, False)
+    swap_arrivals(feat_ref, feat_out, feat_recv)
+    swap_arrivals(up_ref, up_out, up_recv)
 
 
 def forward_exchange(scale, lights, codes, hyper_weight, features, upstream):
@@ -262,8 +275,8 @@
         out_shape=(
             jax.ShapeDtypeStruct((2, chips, block_rows, LANES), jnp.bfloat16),
             jax.ShapeDtypeStruct((chips, depth), jnp.bfloat16),
-            jax.ShapeDtypeStruct((2 * rows + 8, columns, channels), jnp.bfloat16),
-            jax.ShapeDtypeStruct((2 * rows + 4, columns, channels), jnp.bfloat16),
+            jax.ShapeDtypeStruct((2 * rows + HALO, columns, channels), jnp.bfloat16),
+            jax.ShapeDtypeStruct((2 * rows + HALO, columns, channels), jnp.bfloat16),
         ),
         in_specs=[vmem, anywhere, anywhere, anywhere],
         out_specs=(anywhere, vmem, anywhere, anywhere),
@@ -286,7 +299,7 @@
             dma((3,)),
         ],
         compiler_params=pltpu.CompilerParams(
-            has_side_effects=True, vmem_limit_bytes=40 * 1024 * 1024
+            has_side_effects=True, collective_id=0, vmem_limit_bytes=VMEM
         ),
     )(codes, hyper_weight, features, upstream)
 
@@ -348,6 +361,7 @@
     my_group, my_slot = me // GROUP, me % GROUP
     load = pltpu.make_async_copy(parts_ref.at[core], mine, mine_sem)
     load.start()
+    greet()
 
     def to_sibling(group):
         return pltpu.make_async_remote_copy(
@@ -446,50 +460,216 @@
             dma((2,)),
         ],
         compiler_params=pltpu.CompilerParams(
-            has_side_effects=True, vmem_limit_bytes=40 * 1024 * 1024
+            has_side_effects=True, collective_id=1, vmem_limit_bytes=VMEM
         ),
     )(parts, relit, feature_grad)
 
 
-def conv(image, kernel):
-    return lax.conv_general_dilated(
-        image[None],
-        kernel,
-        (1, 1),
-        ((0, 0), (1, 1)),
-        dimension_numbers=("NHWC", "HWIO", "NHWC"),
-        preferred_element_type=jnp.float32,
-    )[0]
-
-
-def conv_back(image, kernel):
-    return lax.conv_general_dilated(
-        image[None],
-        kernel[::-1, ::-1],
-        (1, 1),
-        ((0, 0), (1, 1)),
-        dimension_numbers=("NHWC", "HWOI", "NHWC"),
-        preferred_element_type=jnp.float32,
-    )[0]
-
-
-def kernel_grad(image, upstream):
-    return lax.conv_general_dilated(
-        image[None],
-        upstream[None],
-        (1, 1),
-        ((0, 0), (1, 1)),
-        dimension_numbers=("CHWN", "IHWO", "HWNC"),
-        preferred_element_type=jnp.float32,
+def local_kernel(
+    columns,
+    blocks_ref,
+    feat_ref,
+    up_ref,
+    relit_ref,
+    grad_ref,
+    parts_ref,
+    wide,
+    line,
+    kernels,
+    feats,
+    hidden,
+    grads,
+    slope,
+    total,
+):
+    core = lax.axis_index("tex") % 2
+    frame, channels = feat_ref.shape
+    own = relit_ref.shape[0]
+    rows = frame // columns
+    chips, block_rows = blocks_ref.shape[1], blocks_ref.shape[2]
+    taps = block_rows // 2
+    depth = 9 * channels
+    chunk = total.shape[0]
+    chunk_rows = chunk // columns
+    first_own = pl.multiple_of(core * (frame - own), 16)
+
+    def gather(owner, _):
+        line[...] = blocks_ref[lax.rem(owner, 2), lax.div(owner, 2)].astype(jnp.float32)
+
+        def move(side, _):
+            wide[side, pl.ds(owner * taps, taps), :] = line[pl.ds(side * taps, taps), :]
+            return 0
+
+        return lax.fori_loop(0, 2, move, 0)
+
+    lax.fori_loop(0, 2 * chips, gather, 0)
+
+    def narrow(step, _):
+        span = pl.ds(pl.multiple_of(step * channels, channels), channels)
+        kernels[span, :LANES] = wide[0, span, :].astype(jnp.bfloat16)
+        kernels[span, LANES:] = wide[1, span, :].astype(jnp.bfloat16)
+        return 0
+
+    lax.fori_loop(0, 2 * depth // channels, narrow, 0)
+
+    for image in (feats, hidden, grads):
+        edge = jnp.zeros((columns, image.shape[1]), image.dtype)
+        image[:columns] = edge
+        image[frame + columns :] = edge
+
+    def spread(image, row, values):
+        span = pl.ds(pl.multiple_of((row + 1) * columns, 16), columns)
+        none = jnp.zeros((1, channels), jnp.float32)
+        before = jnp.concatenate([none, values[:-1]], axis=0)
+        after = jnp.concatenate([values[1:], none], axis=0)
+        image[span, :channels] = before.astype(image.dtype)
+        image[span, channels : 2 * channels] = values.astype(image.dtype)
+        image[span, 2 * channels :] = after.astype(image.dtype)
+
+    def row_span(row):
+        return pl.ds(pl.multiple_of(row * columns, 16), columns)
+
+    def place_feats(row, _):
+        spread(feats, row, feat_ref[row_span(row), :].astype(jnp.float32))
+        return 0
+
+    lax.fori_loop(0, rows, place_feats, 0)
+
+    def conv(image, base, start):
+        out = None
+        for tap in range(3):
+            span = pl.ds(pl.multiple_of(start + tap * columns, 16), chunk)
+            piece = jnp.dot(
+                image[span, :],
+                kernels[base + tap * 3 * channels : base + (tap + 1) * 3 * channels, :],
+                preferred_element_type=jnp.float32,
+            )
+            out = piece if out is None else out + piece
+        total[...] = out
+
+    def conv_back(image, base, start):
+        out = None
+        for row_tap in range(3):
+            span = pl.ds(pl.multiple_of(start + (2 - row_tap) * columns, 16), chunk)
+            for col_tap in range(3):
+                at = base + (row_tap * 3 + col_tap) * channels
+                piece = lax.dot_general(
+                    image[span, (2 - col_tap) * channels : (3 - col_tap) * channels],
+                    kernels[at : at + channels, :],
+                    (((1,), (1,)), ((), ())),
+                    preferred_element_type=jnp.float32,
+                )
+                out = piece if out is None else out + piece
+        total[...] = out
+
+    def each_chunk(compute, finish_row):
+        def do_chunk(step, _):
+            compute(step * chunk)
+
+            def do_row(row, _):
+                finish_row(step * chunk_rows + row, total[row_span(row), :])
+                return 0
+
+            return lax.fori_loop(0, chunk_rows, do_row, 0)
+
+        lax.fori_loop(0, frame // chunk, do_chunk, 0)
+
+    def store_own(ref, row, values):
+        local = row - core * (frame - own) // columns
+
+        @pl.when(jnp.logical_and(local >= 0, local < own // columns))
+        def _():
+            ref[row_span(local), :] = values.astype(ref.dtype)
+
+    def end_first(row, pre):
+        sig = jax.nn.sigmoid(pre)
+        slope[row_span(row), :] = sig * (1.0 + pre * (1.0 - sig))
+        spread(hidden, row, pre * sig)
+
+    def end_second(row, pre):
+        sig = jax.nn.sigmoid(pre)
+        store_own(relit_ref, row, pre * sig)
+        up = up_ref[row_span(row), :].astype(jnp.float32)
+        spread(grads, row, up * (sig * (1.0 + pre * (1.0 - sig))))
+
+    def kernel_grad(image, base):
+        upstream = grads[pl.ds(first_own + columns, own), channels : 2 * channels].T
+
+        def do_tap(tap, _):
+            span = pl.ds(pl.multiple_of(first_own + tap * columns, 16), own)
+            for col_tap in range(3):
+                piece = jnp.dot(
+                    upstream,
+                    image[span, col_tap * channels : (col_tap + 1) * channels],
+                    preferred_element_type=jnp.float32,
+                )
+                at = pl.multiple_of(base + (tap * 3 + col_tap) * channels, channels)
+                wide[0, pl.ds(at, channels), :] = piece[:LANES].T
+                wide[1, pl.ds(at, channels), :] = piece[LANES:].T
+            return 0
+
+        lax.fori_loop(0, 3, do_tap, 0)
+
+    def end_grad(row, back):
+        slope[row_span(row), :] = slope[row_span(row), :] * back
+
+    each_chunk(lambda start: conv(feats, 0, start), end_first)
+    each_chunk(lambda start: conv(hidden, depth, start), end_second)
+    each_chunk(lambda start: conv_back(grads, depth, start), end_grad)
+    kernel_grad(hidden, depth)
+
+    def place_grad(row, _):
+        spread(grads, row, slope[row_span(row), :])
+        return 0
+
+    lax.fori_loop(0, rows, place_grad, 0)
+    kernel_grad(feats, 0)
+    each_chunk(
+        lambda start: conv_back(grads, 0, start),
+        lambda row, back: store_own(grad_ref, row, back),
     )
+
+    def scatter(owner, _):
+        def move(side, _):
+            line[pl.ds(side * taps, taps), :] = wide[side, pl.ds(owner * taps, taps), :]
+            return 0
+
+        lax.fori_loop(0, 2, move, 0)
+        parts_ref[lax.rem(owner, 2), lax.div(owner, 2)] = line[...].astype(parts_ref.dtype)
+        return 0
+
+    lax.fori_loop(0, 2 * chips, scatter, 0)
+
+
+def local_work(blocks, feats, upstream, columns):
+    frame, channels = feats.shape
+    own = frame - HALO * columns
+    depth = 9 * channels
+    shifted = pltpu.VMEM((frame + 2 * columns, 3 * channels), jnp.bfloat16)
+    image = jax.ShapeDtypeStruct((own, channels), jnp.bfloat16)
+    return pl.pallas_call(
+        functools.partial(local_kernel, columns),
+        out_shape=(image, image, jax.ShapeDtypeStruct(blocks.shape, jnp.bfloat16)),
+        in_specs=[pl.BlockSpec(memory_space=pltpu.VMEM)] * 3,
+        out_specs=(pl.BlockSpec(memory_space=pltpu.VMEM),) * 3,
+        scratch_shapes=[
+            pltpu.VMEM((2, 2 * depth, LANES), jnp.float32),
+            pltpu.VMEM(blocks.shape[2:], jnp.float32),
+            pltpu.VMEM((2 * depth, channels), jnp.bfloat16),
+            shifted,
+            shifted,
+            shifted,
+            pltpu.VMEM((frame, channels), jnp.float32),
+            pltpu.VMEM((9 * columns, channels), jnp.float32),
+        ],
+        compiler_params=pltpu.CompilerParams(vmem_limit_bytes=VMEM),
+    )(blocks, feats, upstream)
 
 
 def shards(light_ids, tile_offsets, light_table, hyper_weight, features, upstream_grad):
     rows_dev, channels = features.shape[1], features.shape[3]
     scale = 1.0 / math.sqrt(9 * channels)
     lights = lax.axis_size("light")
-    rows = 2 * rows_dev
-    core = lax.axis_index("tex") % 2
     own_codes = light_codes(light_ids, tile_offsets, light_table)
     blocks, codes, feats, upstream = forward_exchange(
         scale,
@@ -501,37 +681,12 @@
     )
     chips = 2 * lights
     taps = hyper_weight.shape[1] // channels
-    kernels = (
-        blocks.reshape(2, chips, 2, taps, LANES)
-        .transpose(1, 0, 3, 2, 4)
-        .reshape(2, 3, 3, channels, channels)
+    columns = feats.shape[1]
+    relit, feature_grad, parts = local_work(
+        blocks, feats.reshape(-1, channels), upstream.reshape(-1, channels), columns
     )
-
-    def inside(values, halo):
-        spot = jnp.arange(rows + 2 * halo) + core * rows - halo
-        kept = jnp.logical_and(spot >= 0, spot < 2 * rows)[:, None, None]
-        return jnp.where(kept, values, jnp.zeros_like(values))
-
-    feats = inside(feats, 4)
-    first_pre = conv(feats, kernels[0])
-    hidden = inside(smooth_act(first_pre), 3).astype(jnp.bfloat16)
-    second_pre = conv(hidden, kernels[1])
-    relit = smooth_act(second_pre[2 : rows + 2]).astype(jnp.bfloat16)
-    second_grad = inside(upstream * smooth_slope(second_pre), 2).astype(jnp.bfloat16)
-    hidden_grad = conv_back(second_grad, kernels[1])
-    first_grad = inside(hidden_grad * smooth_slope(first_pre[2 : rows + 4]), 1).astype(
-        jnp.bfloat16
-    )
-    feature_grad = conv_back(first_grad, kernels[0]).astype(jnp.bfloat16)
-    first_kgrad = kernel_grad(feats[3 : rows + 5], first_grad[1 : rows + 1])
-    second_kgrad = kernel_grad(hidden[2 : rows + 4], second_grad[2 : rows + 2])
-    parts = (
-        jnp.stack([first_kgrad, second_kgrad])
-        .astype(jnp.bfloat16)
-        .reshape(chips, 2, taps, 2, LANES)
-        .transpose(1, 0, 3, 2, 4)
-        .reshape(2, chips, 2 * taps, LANES)
-    )
+    relit = relit.reshape(2 * rows_dev, columns, channels)
+    feature_grad = feature_grad.reshape(2 * rows_dev, columns, channels)
     sums, relit, feature_grad = backward_exchange(lights, parts, relit, feature_grad)
     summed = (
         sums.reshape(chips, 2, taps, LANES).transpose(0, 2, 1, 3).reshape(chips, taps * channels)

time: 242 us -> 149 us (0.62)
  the two profiles are of different devices: /device:TPU:8 before, /device:TPU:1 now
where the time goes in v3:
time: 149 us
  Pallas kernels  138 us (93%)
  local copies, waits for them, and re-layouts  4.87 us (3%)
  matrix products  4.56 us (3%)
    pallas_call x1, Pallas kernels, forward_exchange(): pl.pallas_call(functools.partial(forward_kernel, scale, lights), out_shap...  57.6 us
    pallas_call x1, Pallas kernels, backward_exchange(): pl.pallas_call(functools.partial(backward_kernel, lights), out_shape=(jax...  42.6 us
    pallas_call x1, Pallas kernels, local_work(): pl.pallas_call(functools.partial(local_kernel, columns), out_shape=(image...  37.5 us
    dot_general x1, matrix products, shards(): jnp.einsum('lz,ls->zs', codes, summed, preferred_element_type=jnp.float32)  3.6 us

profile of v3, /device:TPU:1, one launch (start us, length us, event | category | flops | bytes accessed | tf_op | source)
XLA Modules:
  0.0 148.8 jit_solution(13123266760446687532)
XLA Ops:
  0.6 0.0 copy-start
  0.6 0.7 convert_element_type.11
  1.4 0.1 multiply_sine_fusion
  1.5 0.1 copy-done
  1.6 1.0 multiply_reduce_fusion
  2.6 0.1 fusion.2
  2.6 0.6 reshape.53.codes_ref
  3.3 57.6 %shard_map.85 = (bf16[2,128,36,128]{3,2,1,0:T(8,128)(2,1)}, bf16[128,512]{1,0:T(8,128)(2,1)}, bf16[36,48,256]{2,1,0:T(8,128)(2,1)}, bf16[36,48,256]{2,1,0:T(8,128)(2,1)}) custom-call(f32[8,128]{1,0:T(8,128)} %reshape.53.codes_ref, bf16[512,4608]{1,0:T(8,128)(2,1)} %hyper_ref.1, bf16[2,16,48,256]{3,2,1,0:T(8,128)(2,1)} %feat_ref.1, ...), custom_call_target="tpu_custom_call" | custom-call | tf_op jit(solution)/shard_map/pallas_call | solution.py:273
  60.8 37.5 %shard_map.86 = (bf16[1536,256]{1,0:T(8,128)(2,1)}, bf16[1536,256]{1,0:T(8,128)(2,1)}, bf16[2,128,36,128]{3,2,1,0:T(8,128)(2,1)}) custom-call(bf16[2,128,36,128]{3,2,1,0:T(8,128)(2,1)} %get-tuple-element.13.blocks_ref, bf16[1728,256]{1,0:T(8,128)(2,1)} %bitcast.13, bf16[1728,256]{1,0:T(8,128)(2,1)} %bitcast.14), custom_call_target="tpu_custom_call" | custom-call | tf_op jit(solution)/shard_map/pallas_call | solution.py:650
  98.4 42.6 %shard_map.87 = (bf16[128,36,128]{2,1,0:T(8,128)(2,1)}, bf16[2,16,48,256]{3,2,1,0:T(8,128)(2,1)}, bf16[2,16,48,256]{3,2,1,0:T(8,128)(2,1)}) custom-call(bf16[2,128,36,128]{3,2,1,0:T(8,128)(2,1)} %get-tuple-element.16.parts_ref, bf16[32,48,256]{2,1,0:T(8,128)(2,1)} %bitcast.15, bf16[32,48,256]{2,1,0:T(8,128)(2,1)} %bitcast.16), custom_call_target="tpu_custom_call" | custom-call | tf_op jit(solution)/shard_map/pallas_call | solution.py:438
  141.0 0.0 copy-start.3
  141.0 1.6 %copy.9 = bf16[128,36,128]{2,0,1:T(8,128)(2,1)S(1)} copy(bf16[128,36,128]{2,1,0:T(8,128)(2,1)} %get-tuple-element.22) | data formatting | bytes 2359296 | tf_op jit(solution)/shard_map/pallas_call | solution.py:438
  142.7 0.7 copy.10
  143.4 0.0 copy-done.3
  143.4 0.0 copy-start.2
  143.4 0.0 copy-start.1
  143.4 3.6 %multiply_convert_fusion = bf16[512,4608]{1,0:T(8,128)(2,1)} fusion(bf16[128,512]{1,0:T(8,128)(2,1)S(1)} %copy-done.3, bf16[128,4608]{0,1:T(8,128)(2,1)S(1)} %bitcast.12), kind=kOutput, calls=%fused_computation | convolution fusion | flops 608698368 | bytes 6029312 | tf_op jit(solution)/shard_map/lz,ls->zs/dot_general | solution.py:695
  147.0 0.0 copy-done.2
  147.0 0.9 copy.13
  147.9 0.0 copy-done.1
  147.9 0.9 copy.14
  (2 shorter events, 0.0 us)
Async XLA Ops:
  0.6 1.0 copy-start
  141.0 2.4 %copy-start.3 = (bf16[128,512]{1,0:T(8,128)(2,1)S(1)}, bf16[128,512]{1,0:T(8,128)(2,1)}, u32[]{:S(2)}) copy-start(bf16[128,512]{1,0:T(8,128)(2,1)} %get-tuple-element.21) | copy-start | bytes 393220
  143.4 3.6 %copy-start.2 = (bf16[2,16,48,256]{3,2,1,0:T(8,128)(2,1)S(1)}, bf16[2,16,48,256]{3,2,1,0:T(8,128)(2,1)}, u32[]{:S(2)}) copy-start(bf16[2,16,48,256]{3,2,1,0:T(8,128)(2,1)} %get-tuple-element.30) | copy-start | bytes 2359300
  143.4 4.5 %copy-start.1 = (bf16[2,16,48,256]{3,2,1,0:T(8,128)(2,1)S(1)}, bf16[2,16,48,256]{3,2,1,0:T(8,128)(2,1)}, u32[]{:S(2)}) copy-start(bf16[2,16,48,256]{3,2,1,0:T(8,128)(2,1)} %get-tuple-element.31) | copy-start | bytes 2359300

commit v4 on v0

v4 whole, which is shorter than its diff:
```python
import functools
import math

import jax
import jax.numpy as jnp
from jax import lax
from jax.experimental import pallas as pl
from jax.experimental.pallas import tpu as pltpu
from jax.sharding import PartitionSpec as P

MESH = pl.DeviceIdType.MESH
LANES = 128
GROUP = 16
HALO = 4
VMEM = 60 * 1024 * 1024


def light_codes(light_ids, tile_offsets, light_table):
    halfway = light_table.shape[1] // 2
    onehot = (
        light_ids[:, None] == jnp.arange(light_table.shape[0], dtype=jnp.int32)[None, :]
    ).astype(jnp.bfloat16)
    looked = jnp.dot(onehot, light_table, preferred_element_type=jnp.float32)
    rates = jnp.exp(-math.log(1000.0) * jnp.arange(halfway, dtype=jnp.float32) / halfway)
    angles = tile_offsets.astype(jnp.float32)[:, None] * rates[None, :]
    summed = looked + jnp.concatenate([jnp.sin(angles), jnp.cos(angles)], axis=1)
    return (summed * lax.rsqrt(jnp.mean(summed * summed, axis=1, keepdims=True) + 1e-06)).astype(
        jnp.bfloat16
    )


def place():
    light, tex = lax.axis_index("light"), lax.axis_index("tex")
    half, core = tex // 2, tex % 2
    return light, half, core, light * 2 + half


def peer(chip, core):
    return (chip // 2, (chip % 2) * 2 + core)


def greet():
    light, half, core, me = place()
    chips = 2 * lax.axis_size("light")
    barrier = pltpu.get_barrier_semaphore()

    def signal(target):
        pl.semaphore_signal(barrier, inc=1, device_id=target, device_id_type=MESH)

    def signal_chip(step, _):
        signal(peer(lax.rem(me + step, chips), core))
        return 0

    lax.fori_loop(1, chips, signal_chip, 0)
    signal((light, half * 2 + 1 - core))
    signal((light, (1 - half) * 2 + 1 - core))
    pl.semaphore_wait(barrier, chips + 1)


def await_bytes(ref, sem):
    pltpu.make_async_copy(ref, ref, sem).wait()


def swap_copies(src, dst, send, recv, start):
    light, half, core, _ = place()
    rows = src.shape[1]
    halo = dst.shape[0] - 2 * rows

    def go(source, target, to_half, to_core, slot, number):
        here = jnp.logical_and(to_half == half, to_core == core)

        @pl.when(here)
        def _():
            if start:
                pltpu.make_async_copy(source, target, recv.at[slot]).start()

        @pl.when(jnp.logical_not(here))
        def _():
            copy = pltpu.make_async_remote_copy(
                src_ref=source,
                dst_ref=target,
                send_sem=send.at[number],
                recv_sem=recv.at[slot],
                device_id=(light, to_half * 2 + to_core),
                device_id_type=MESH,
            )
            if start:
                copy.start()
            else:
                copy.wait_send()

    for to_half in range(2):
        for own in range(2):

            @pl.when(core == own)
            def _():
                go(
                    src.at[to_half],
                    dst.at[pl.ds(own * rows + halo * half, rows)],
                    to_half,
                    half,
                    own,
                    to_half,
                )

        @pl.when(jnp.logical_and(half == 1, core == 0))
        def _():
            go(
                src.at[to_half, pl.ds(0, halo)],
                dst.at[pl.ds(2 * rows, halo)],
                to_half,
                0,
                2,
                2 + to_half,
            )

        @pl.when(jnp.logical_and(half == 0, core == 1))
        def _():
            go(
                src.at[to_half, pl.ds(rows - halo, halo)],
                dst.at[pl.ds(0, halo)],
                to_half,
                1,
                2,
                2 + to_half,
            )


def swap_arrivals(src, dst, recv):
    rows = src.shape[1]
    halo = dst.shape[0] - 2 * rows
    for slot, count in ((0, rows), (1, rows), (2, halo)):
        await_bytes(dst.at[pl.ds(0, count)], recv.at[slot])


def give_back(src, dst, send, recv, start):
    light, half, core, _ = place()
    rows = dst.shape[1]
    for piece in range(2):
        here = jnp.logical_and(core == half, piece == core)
        source = src.at[pl.ds(piece * rows, rows)]
        for own in range(2):

            @pl.when(jnp.logical_and(here, half == own))
            def _():
                if start:
                    pltpu.make_async_copy(source, dst.at[own], recv.at[own]).start()

            @pl.when(jnp.logical_and(jnp.logical_not(here), half == own))
            def _():
                copy = pltpu.make_async_remote_copy(
                    src_ref=source,
                    dst_ref=dst.at[own],
                    send_sem=send.at[piece],
                    recv_sem=recv.at[own],
                    device_id=(light, core * 2 + piece),
                    device_id_type=MESH,
                )
                if start:
                    copy.start()
                else:
                    copy.wait_send()


def whole_kernel(
    scale,
    lights,
    codes_ref,
    hyper_ref,
    feat_ref,
    up_ref,
    codes_out,
    sums_ref,
    relit_out,
    grad_out,
    hyper,
    codes,
    table,
    ready,
    blocks,
    wide,
    line,
    kernels,
    feat,
    up,
    feats,
    hidden,
    grads,
    slope,
    total,
    relit,
    grad,
    parts,
    theirs,
    added,
    hyper_sem,
    code_send,
    code_recv,
    own_sem,
    block_send,
    block_recv,
    pass_send,
    pass_recv,
    feat_send,
    feat_recv,
    up_send,
    up_recv,
    core_send,
    core_recv,
    sum_send,
    sum_recv,
    relit_send,
    relit_recv,
    grad_send,
    grad_recv,
):
    light, half, core, me = place()
    chips = 2 * lights
    groups = chips // GROUP
    my_group, my_slot = me // GROUP, me % GROUP
    sibling = (light, half * 2 + 1 - core)
    block_rows = ready.shape[1]
    taps = block_rows // 2
    rows, columns, channels = feat.shape
    own_rows = relit.shape[0]
    frame, own = rows * columns, own_rows * columns
    depth = 9 * channels
    chunk = total.shape[0]
    chunk_rows = chunk // columns
    inner = rows - own_rows
    first_own = pl.multiple_of(core * inner * columns, 16)

    load = pltpu.make_async_copy(hyper_ref, hyper, hyper_sem)
    load.start()
    greet()

    mine = pl.ds(pl.multiple_of(light * 8, 8), 8)
    codes[mine, :] = codes_ref[...]

    def send_codes(step, _):
        pltpu.make_async_remote_copy(
            src_ref=codes_ref,
            dst_ref=codes.at[mine],
            send_sem=code_send,
            recv_sem=code_recv,
            device_id=(lax.rem(light + step, lights), half * 2 + core),
            device_id_type=MESH,
        ).start()
        return 0

    lax.fori_loop(1, lights, send_codes, 0)
    swap_copies(feat_ref, feat, feat_send, feat_recv, True)
    swap_copies(up_ref, up, up_send, up_recv, True)
    for image in (feats, hidden, grads):
        edge = jnp.zeros((columns, image.shape[1]), image.dtype)
        image[:columns] = edge
        image[frame + columns :] = edge
    arrived = codes.at[pl.ds(0, 8 * (lights - 1))]
    await_bytes(arrived, code_recv)
    all_codes = jnp.concatenate(
        [codes[pl.ds(k, chips, stride=4), :] for k in range(4)], axis=1
    ).astype(jnp.bfloat16)
    codes_out[...] = all_codes
    load.wait()

    for row in range(taps):
        product = scale * jnp.dot(
            all_codes,
            hyper[:, row * 2 * LANES : (row + 1) * 2 * LANES],
            preferred_element_type=jnp.float32,
        )
        table[pl.ds(row, chips, stride=40), :] = product[:, :LANES]
        table[pl.ds(taps + row, chips, stride=40), :] = product[:, LANES:]

    def narrow(chip):
        ready[chip] = table[pl.ds(pl.multiple_of(chip * 40, 8), block_rows), :].astype(
            jnp.bfloat16
        )

    narrow(me)
    keep = pltpu.make_async_copy(ready.at[me], blocks.at[core, me], own_sem)
    keep.start()

    def send_block(step, _):
        group = lax.rem(my_group + step // GROUP, groups)
        other = group * GROUP + lax.rem(my_slot + step % GROUP, GROUP)
        narrow(other)
        pltpu.make_async_remote_copy(
            src_ref=ready.at[other],
            dst_ref=blocks.at[core, me],
            send_sem=block_send,
            recv_sem=block_recv.at[my_group],
            device_id=peer(other, core),
            device_id_type=MESH,
        ).start()
        return 0

    lax.fori_loop(1, chips, send_block, 0)

    def row_span(row):
        return pl.ds(pl.multiple_of(row * columns, 16), columns)

    def spread(image, row, values):
        span = row_span(row + 1)
        none = jnp.zeros((1, channels), jnp.float32)
        before = jnp.concatenate([none, values[:-1]], axis=0)
        after = jnp.concatenate([values[1:], none], axis=0)
        image[span, :channels] = before.astype(image.dtype)
        image[span, channels : 2 * channels] = values.astype(image.dtype)
        image[span, 2 * channels :] = after.astype(image.dtype)

    swap_arrivals(feat_ref, feat, feat_recv)
    swap_arrivals(up_ref, up, up_recv)

    def place_feats(row, _):
        spread(feats, row, feat[row].astype(jnp.float32))
        return 0

    lax.fori_loop(0, rows, place_feats, 0)

    def to_sibling(group):
        span = blocks.at[core, pl.ds(group * GROUP, GROUP)]
        return pltpu.make_async_remote_copy(
            src_ref=span,
            dst_ref=span,
            send_sem=pass_send.at[group],
            recv_sem=pass_recv.at[group],
            device_id=sibling,
            device_id_type=MESH,
        )

    def gather(group, from_core):
        def block(slot, _):
            chip = group * GROUP + slot
            line[...] = blocks[from_core, chip].astype(jnp.float32)

            def move(side, _):
                wide[side, pl.ds((2 * chip + from_core) * taps, taps), :] = line[
                    pl.ds(side * taps, taps), :
                ]
                return 0

            return lax.fori_loop(0, 2, move, 0)

        lax.fori_loop(0, GROUP, block, 0)

    def end_group(group):
        to_sibling(group).wait_recv()
        gather(group, 1 - core)
        count = 2 * GROUP * taps
        span = pl.ds(pl.multiple_of(group * count, 16), count)
        kernels[span, :LANES] = wide[0, span, :].astype(jnp.bfloat16)
        kernels[span, LANES:] = wide[1, span, :].astype(jnp.bfloat16)

    keep.wait()
    await_bytes(blocks.at[core, pl.ds(0, GROUP - 1)], block_recv.at[my_group])
    to_sibling(my_group).start()
    gather(my_group, core)

    def take_group(step, _):
        group = lax.rem(my_group + groups - step, groups)
        await_bytes(blocks.at[core, pl.ds(0, GROUP)], block_recv.at[group])
        to_sibling(group).start()
        gather(group, core)
        end_group(lax.rem(group + 1, groups))
        return 0

    lax.fori_loop(1, groups, take_group, 0)
    end_group(lax.rem(my_group + 1, groups))

    def conv(image, base, start):
        out = None
        for tap in range(3):
            span = pl.ds(pl.multiple_of(start + tap * columns, 16), chunk)
            piece = jnp.dot(
                image[span, :],
                kernels[base + tap * 3 * channels : base + (tap + 1) * 3 * channels, :],
                preferred_element_type=jnp.float32,
            )
            out = piece if out is None else out + piece
        total[...] = out

    def conv_back(image, base, start):
        out = None
        for row_tap in range(3):
            span = pl.ds(pl.multiple_of(start + (2 - row_tap) * columns, 16), chunk)
            for col_tap in range(3):
                at = base + (row_tap * 3 + col_tap) * channels
                piece = lax.dot_general(
                    image[span, (2 - col_tap) * channels : (3 - col_tap) * channels],
                    kernels[at : at + channels, :],
                    (((1,), (1,)), ((), ())),
                    preferred_element_type=jnp.float32,
                )
                out = piece if out is None else out + piece
        total[...] = out

    def each_chunk(compute, finish_row):
        def do_chunk(step, _):
            compute(step * chunk)

            def do_row(row, _):
                finish_row(step * chunk_rows + row, total[row_span(row), :])
                return 0

            return lax.fori_loop(0, chunk_rows, do_row, 0)

        lax.fori_loop(0, frame // chunk, do_chunk, 0)

    def store_own(ref, row, values):
        local = row - core * inner

        @pl.when(jnp.logical_and(local >= 0, local < own_rows))
        def _():
            ref[local] = values.astype(ref.dtype)

    def end_first(row, pre):
        sig = jax.nn.sigmoid(pre)
        slope[row_span(row), :] = sig * (1.0 + pre * (1.0 - sig))
        spread(hidden, row, pre * sig)

    def end_second(row, pre):
        sig = jax.nn.sigmoid(pre)
        store_own(relit, row, pre * sig)
        spread(grads, row, up[row].astype(jnp.float32) * (sig * (1.0 + pre * (1.0 - sig))))

    def kernel_grad(image, base):
        upstream = grads[pl.ds(first_own + columns, own), channels : 2 * channels].T

        def do_tap(tap, _):
            span = pl.ds(pl.multiple_of(first_own + tap * columns, 16), own)
            for col_tap in range(3):
                piece = jnp.dot(
                    upstream,
                    image[span, col_tap * channels : (col_tap + 1) * channels],
                    preferred_element_type=jnp.float32,
                )
                at = pl.multiple_of(base + (tap * 3 + col_tap) * channels, channels)
                wide[0, pl.ds(at, channels), :] = piece[:LANES].T
                wide[1, pl.ds(at, channels), :] = piece[LANES:].T
            return 0

        lax.fori_loop(0, 3, do_tap, 0)

    def end_grad(row, back):
        slope[row_span(row), :] = slope[row_span(row), :] * back

    def part_copy(group):
        return pltpu.make_async_remote_copy(
            src_ref=parts.at[pl.ds(group * GROUP, GROUP)],
            dst_ref=theirs.at[pl.ds(group * GROUP, GROUP)],
            send_sem=core_send.at[group],
            recv_sem=core_recv.at[group],
            device_id=sibling,
            device_id_type=MESH,
        )

    def pick(owner):
        def move(side, _):
            line[pl.ds(side * taps, taps), :] = wide[side, pl.ds(owner * taps, taps), :]
            return 0

        lax.fori_loop(0, 2, move, 0)
        return line[...]

    def send_grad(first):
        some = groups // 2

        def group_at(step):
            return first + lax.rem(my_group + step, some)

        def share(step):
            group = group_at(step)

            def block(slot, _):
                chip = group * GROUP + slot
                parts[chip] = pick(2 * chip + 1 - core).astype(parts.dtype)
                return 0

            lax.fori_loop(0, GROUP, block, 0)
            part_copy(group).start()

        def add(step):
            group = group_at(step)
            part_copy(group).wait_recv()

            def block(slot, _):
                other = group * GROUP + lax.rem(my_slot + slot, GROUP)
                added[other] = (
                    pick(2 * other + core) + theirs[other].astype(jnp.float32)
                ).astype(added.dtype)

                @pl.when(other != me)
                def _():
                    pltpu.make_async_remote_copy(
                        src_ref=added.at[other],
                        dst_ref=sums_ref.at[me],
                        send_sem=sum_send,
                        recv_sem=sum_recv,
                        device_id=peer(other, core),
                        device_id_type=MESH,
                    ).start()

                return 0

            lax.fori_loop(0, GROUP, block, 0)

        share(0)

        def both(step, _):
            share(step)
            add(step - 1)
            return 0

        lax.fori_loop(1, some, both, 0)
        add(some - 1)

    each_chunk(lambda start: conv(feats, 0, start), end_first)
    each_chunk(lambda start: conv(hidden, depth, start), end_second)
    kernel_grad(hidden, depth)
    send_grad(groups // 2)
    give_back(relit, relit_out, relit_send, relit_recv, True)
    each_chunk(lambda start: conv_back(grads, depth, start), end_grad)

    def place_grad(row, _):
        spread(grads, row, slope[row_span(row), :])
        return 0

    lax.fori_loop(0, rows, place_grad, 0)
    kernel_grad(feats, 0)
    send_grad(0)
    each_chunk(
        lambda start: conv_back(grads, 0, start),
        lambda row, back: store_own(grad, row, back),
    )
    give_back(grad, grad_out, grad_send, grad_recv, True)
    last = pltpu.make_async_copy(added.at[me], sums_ref.at[me], own_sem)
    last.start()

    def finish(group, _):
        to_sibling(group).wait_send()
        part_copy(group).wait_send()
        return 0

    lax.fori_loop(0, groups, finish, 0)
    await_bytes(ready.at[pl.ds(0, chips - 1)], block_send)
    await_bytes(arrived, code_send)
    swap_copies(feat_ref, feat, feat_send, feat_recv, False)
    swap_copies(up_ref, up, up_send, up_recv, False)
    give_back(relit, relit_out, relit_send, relit_recv, False)
    give_back(grad, grad_out, grad_send, grad_recv, False)
    for slot in range(2):
        await_bytes(relit_out.at[slot], relit_recv.at[slot])
        await_bytes(grad_out.at[slot], grad_recv.at[slot])
    last.wait()
    await_bytes(added.at[pl.ds(0, chips - 1)], sum_send)
    await_bytes(sums_ref.at[pl.ds(0, chips - 1)], sum_recv)


def whole(scale, lights, codes, hyper_weight, features, upstream):
    chips = 2 * lights
    groups = chips // GROUP
    width, own_len = hyper_weight.shape
    block_rows = own_len // LANES
    _, rows_dev, columns, channels = features.shape
    depth = 9 * channels
    own_rows = 2 * rows_dev
    rows = own_rows + HALO
    frame = rows * columns
    dma = pltpu.SemaphoreType.DMA
    anywhere = pl.BlockSpec(memory_space=pl.ANY)
    vmem = pl.BlockSpec(memory_space=pltpu.VMEM)
    image = jax.ShapeDtypeStruct(features.shape, jnp.bfloat16)
    block = pltpu.VMEM((chips, block_rows, LANES), jnp.bfloat16)
    shifted = pltpu.VMEM((frame + 2 * columns, 3 * channels), jnp.bfloat16)
    return pl.pallas_call(
        functools.partial(whole_kernel, scale, lights),
        out_shape=(
            jax.ShapeDtypeStruct((chips, width), jnp.bfloat16),
            jax.ShapeDtypeStruct((chips, block_rows, LANES), jnp.bfloat16),
            image,
            image,
        ),
        in_specs=[vmem, anywhere, anywhere, anywhere],
        out_specs=(vmem, anywhere, anywhere, anywhere),
        scratch_shapes=[
            pltpu.VMEM((width, own_len), jnp.bfloat16),
            pltpu.VMEM((8 * lights, LANES), jnp.float32),
            pltpu.VMEM((chips * 40, LANES), jnp.float32),
            block,
            pltpu.VMEM((2, chips, block_rows, LANES), jnp.bfloat16),
            pltpu.VMEM((2, 2 * depth, LANES), jnp.float32),
            pltpu.VMEM((block_rows, LANES), jnp.float32),
            pltpu.VMEM((2 * depth, channels), jnp.bfloat16),
            pltpu.VMEM((rows, columns, channels), jnp.bfloat16),
            pltpu.VMEM((rows, columns, channels), jnp.bfloat16),
            shifted,
            shifted,
            shifted,
            pltpu.VMEM((frame, channels), jnp.float32),
            pltpu.VMEM((9 * columns, channels), jnp.float32),
            pltpu.VMEM((own_rows, columns, channels), jnp.bfloat16),
            pltpu.VMEM((own_rows, columns, channels), jnp.bfloat16),
            block,
            block,
            block,
            dma,
            dma,
            dma,
            dma,
            dma,
            dma((groups,)),
            dma((groups,)),
            dma((groups,)),
            dma((4,)),
            dma((3,)),
            dma((4,)),
            dma((3,)),
            dma((groups,)),
            dma((groups,)),
            dma,
            dma,
            dma((2,)),
            dma((2,)),
            dma((2,)),
            dma((2,)),
        ],
        compiler_params=pltpu.CompilerParams(
            has_side_effects=True, collective_id=0, vmem_limit_bytes=VMEM
        ),
    )(codes, hyper_weight, features, upstream)


def shards(light_ids, tile_offsets, light_table, hyper_weight, features, upstream_grad):
    channels = features.shape[3]
    scale = 1.0 / math.sqrt(9 * channels)
    lights = lax.axis_size("light")
    own_codes = light_codes(light_ids, tile_offsets, light_table)
    codes, sums, relit, feature_grad = whole(
        scale,
        lights,
        own_codes.astype(jnp.float32).reshape(8, LANES),
        hyper_weight,
        features,
        upstream_grad,
    )
    chips = 2 * lights
    taps = hyper_weight.shape[1] // channels
    summed = (
        sums.reshape(chips, 2, taps, LANES).transpose(0, 2, 1, 3).reshape(chips, taps * channels)
    )
    hyper_grad = (
        scale * jnp.einsum("lz,ls->zs", codes, summed, preferred_element_type=jnp.float32)
    ).astype(jnp.bfloat16)
    return (relit, feature_grad, hyper_grad)


def solution(mesh):
    in_specs = (
        P("light"),
        P("light"),
        P(),
        P(None, ("light", "tex")),
        P("light", "tex", None, None),
        P("light", "tex", None, None),
    )
    out_specs = (
        P("light", "tex", None, None),
        P("light", "tex", None, None),
        P(None, ("light", "tex")),
    )
    return jax.shard_map(shards, mesh=mesh, in_specs=in_specs, out_specs=out_specs, check_vma=False)
```

time: 615 us -> 120 us (0.20); the launches traced: 608 us -> 120 us
  blocking collectives: 245 us -> 0 us
  waiting for transfers between devices: 188 us -> 0 us
  Pallas kernels: 0 us -> 109 us
  local copies, waits for them, and re-layouts: 62 us -> 4.87 us
  starting transfers between devices: 43.7 us -> 0 us
  matrix products: 38.3 us -> 4.56 us
  other arithmetic: 16.2 us -> 0.91 us
  between operations: 14.8 us -> 0.71 us
    all_gather x1 -> x0, blocking collectives: 133 us -> none  [shards(): all_codes = lax.all_gather(own_codes, 'light', axis=0, tiled=True)]
    all_to_all x1 -> x0, blocking collectives: 112 us -> none  [shards(): lax.all_to_all(grads.astype(jnp.bfloat16), 'light', split_axis=1, concat_...]
    pallas_call x0 -> x1, Pallas kernels: none -> 109 us  [whole(): pl.pallas_call(functools.partial(whole_kernel, scale, lights), out_shape=...]
    all_to_all x1 -> x0, waiting for transfers between devices: 77.5 us -> none  [shards(): lax.all_to_all(quarters, 'light', split_axis=0, concat_axis=1, tiled=True)]
    all_gather x1 -> x0, waiting for transfers between devices: 65.8 us -> none  [shards(): quarters = lax.all_gather(columns, 'tex', axis=1, tiled=True)]
    reduce_scatter x1 -> x0, waiting for transfers between devices: 37 us -> none  [shards(): lax.psum_scatter(spread.astype(jnp.bfloat16), 'tex', scatter_dimension=1,...]
    dot_general x8 -> x1, matrix products: 37.3 us -> 3.61 us  [shards(): jnp.einsum('lz,ls->zs', codes, summed, preferred_element_type=jnp.float32)]
    ppermute x8 -> x0, starting transfers between devices: 33.1 us -> none  [the longest x4 24.9 us: padded_2(): lax.ppermute(lax.slice_in_dim(block, block.shape[dim] - width, None, axis...]
  transfers between devices with their start and end apart: 11 -> 0, of which waited for: 5 -> 0; matrix products, arithmetic and copies ran while one was open for 7% -> 0% of each run, Pallas kernels for 0% -> 0%
where the time goes in v4:
time: 120 us
  Pallas kernels  109 us (91%)
  local copies, waits for them, and re-layouts  4.87 us (4%)
  matrix products  4.56 us (4%)
    pallas_call x1, Pallas kernels, whole(): pl.pallas_call(functools.partial(whole_kernel, scale, lights), out_shape=...  109 us
    dot_general x1, matrix products, shards(): jnp.einsum('lz,ls->zs', codes, summed, preferred_element_type=jnp.float32)  3.61 us

profile of v4, /device:TPU:1, one launch (start us, length us, event | category | flops | bytes accessed | tf_op | source)
XLA Modules:
  0.0 119.7 jit_solution(13442694294378792053)
XLA Ops:
  0.6 0.0 copy-start
  0.6 0.7 convert_element_type.11
  1.4 0.1 multiply_sine_fusion
  1.5 0.1 copy-done
  1.6 1.0 multiply_reduce_fusion
  2.6 0.1 fusion.2
  2.6 0.6 reshape.37.codes_ref
  3.3 108.6 %shard_map.85 = (bf16[128,512]{1,0:T(8,128)(2,1)}, bf16[128,36,128]{2,1,0:T(8,128)(2,1)}, bf16[2,16,48,256]{3,2,1,0:T(8,128)(2,1)}, bf16[2,16,48,256]{3,2,1,0:T(8,128)(2,1)}) custom-call(f32[8,128]{1,0:T(8,128)} %reshape.37.codes_ref, bf16[512,4608]{1,0:T(8,128)(2,1)} %hyper_ref.1, bf16[2,16,48,256]{3,2,1,0:T(8,128)(2,1)} %feat_ref.1, ...), custom_call_target="tpu_custom_call" | custom-call | tf_op jit(solution)/shard_map/pallas_call | solution.py:576
  111.9 0.0 copy-start.3
  111.9 1.6 %copy.9 = bf16[128,36,128]{2,0,1:T(8,128)(2,1)S(1)} copy(bf16[128,36,128]{2,1,0:T(8,128)(2,1)} %get-tuple-element.10) | data formatting | bytes 2359296 | tf_op jit(solution)/shard_map/pallas_call | solution.py:576
  113.5 0.7 copy.10
  114.3 0.0 copy-start.2
  114.3 0.0 copy-done.3
  114.3 0.0 copy-start.1
  114.3 3.6 %multiply_convert_fusion = bf16[512,4608]{1,0:T(8,128)(2,1)} fusion(bf16[128,512]{1,0:T(8,128)(2,1)S(1)} %copy-done.3, bf16[128,4608]{0,1:T(8,128)(2,1)S(1)} %bitcast.8), kind=kOutput, calls=%fused_computation | convolution fusion | flops 608698368 | bytes 6029312 | tf_op jit(solution)/shard_map/lz,ls->zs/dot_general | solution.py:653
  117.9 0.0 copy-done.2
  117.9 0.9 copy.13
  118.8 0.0 copy-done.1
  118.8 0.9 copy.14
  (2 shorter events, 0.0 us)
Async XLA Ops:
  0.6 1.0 copy-start
  111.9 2.4 %copy-start.3 = (bf16[128,512]{1,0:T(8,128)(2,1)S(1)}, bf16[128,512]{1,0:T(8,128)(2,1)}, u32[]{:S(2)}) copy-start(bf16[128,512]{1,0:T(8,128)(2,1)} %get-tuple-element.9) | copy-start | bytes 393220
  114.3 3.6 %copy-start.2 = (bf16[2,16,48,256]{3,2,1,0:T(8,128)(2,1)S(1)}, bf16[2,16,48,256]{3,2,1,0:T(8,128)(2,1)}, u32[]{:S(2)}) copy-start(bf16[2,16,48,256]{3,2,1,0:T(8,128)(2,1)} %get-tuple-element.18) | copy-start | bytes 2359300
  114.3 4.5 %copy-start.1 = (bf16[2,16,48,256]{3,2,1,0:T(8,128)(2,1)S(1)}, bf16[2,16,48,256]{3,2,1,0:T(8,128)(2,1)}, u32[]{:S(2)}) copy-start(bf16[2,16,48,256]{3,2,1,0:T(8,128)(2,1)} %get-tuple-element.19) | copy-start | bytes 2359300

commit v5 on v4

--- a/solution.py
+++ b/solution.py
@@ -12,6 +12,8 @@
 LANES = 128
 GROUP = 16
 HALO = 4
+PIECES = 4
+CHUNK_ROWS = 18
 VMEM = 60 * 1024 * 1024
 
 
@@ -133,33 +135,34 @@
         await_bytes(dst.at[pl.ds(0, count)], recv.at[slot])
 
 
-def give_back(src, dst, send, recv, start):
+def give_back(src, dst, send, recv, piece, start):
     light, half, core, _ = place()
-    rows = dst.shape[1]
-    for piece in range(2):
-        here = jnp.logical_and(core == half, piece == core)
-        source = src.at[pl.ds(piece * rows, rows)]
-        for own in range(2):
-
-            @pl.when(jnp.logical_and(here, half == own))
-            def _():
-                if start:
-                    pltpu.make_async_copy(source, dst.at[own], recv.at[own]).start()
-
-            @pl.when(jnp.logical_and(jnp.logical_not(here), half == own))
-            def _():
-                copy = pltpu.make_async_remote_copy(
-                    src_ref=source,
-                    dst_ref=dst.at[own],
-                    send_sem=send.at[piece],
-                    recv_sem=recv.at[own],
-                    device_id=(light, core * 2 + piece),
-                    device_id_type=MESH,
-                )
-                if start:
-                    copy.start()
-                else:
-                    copy.wait_send()
+    count = src.shape[0] // PIECES
+    to_core, part = piece // (PIECES // 2), piece % (PIECES // 2)
+    here = jnp.logical_and(core == half, to_core == core)
+    source = src.at[pl.ds(piece * count, count)]
+    target = dst.at[half, pl.ds(part * count, count)]
+    slot = half * (PIECES // 2) + part
+
+    @pl.when(here)
+    def _():
+        if start:
+            pltpu.make_async_copy(source, target, recv.at[slot]).start()
+
+    @pl.when(jnp.logical_not(here))
+    def _():
+        copy = pltpu.make_async_remote_copy(
+            src_ref=source,
+            dst_ref=target,
+            send_sem=send.at[piece],
+            recv_sem=recv.at[slot],
+            device_id=(light, core * 2 + to_core),
+            device_id_type=MESH,
+        )
+        if start:
+            copy.start()
+        else:
+            copy.wait_send()
 
 
 def whole_kernel(
@@ -170,7 +173,7 @@
     feat_ref,
     up_ref,
     codes_out,
-    sums_ref,
+    summed_out,
     relit_out,
     grad_out,
     hyper,
@@ -193,6 +196,7 @@
     parts,
     theirs,
     added,
+    sums,
     hyper_sem,
     code_send,
     code_recv,
@@ -380,10 +384,10 @@
             out = piece if out is None else out + piece
         total[...] = out
 
-    def conv_back(image, base, start):
+    def conv_back(image, base, start, count):
         out = None
         for row_tap in range(3):
-            span = pl.ds(pl.multiple_of(start + (2 - row_tap) * columns, 16), chunk)
+            span = pl.ds(pl.multiple_of(start + (2 - row_tap) * columns, 16), count)
             for col_tap in range(3):
                 at = base + (row_tap * 3 + col_tap) * channels
                 piece = lax.dot_general(
@@ -393,7 +397,7 @@
                     preferred_element_type=jnp.float32,
                 )
                 out = piece if out is None else out + piece
-        total[...] = out
+        total[:count] = out
 
     def each_chunk(compute, finish_row):
         def do_chunk(step, _):
@@ -463,7 +467,7 @@
         lax.fori_loop(0, 2, move, 0)
         return line[...]
 
-    def send_grad(first):
+    def send_grad(first, between):
         some = groups // 2
 
         def group_at(step):
@@ -490,13 +494,17 @@
                     pick(2 * other + core) + theirs[other].astype(jnp.float32)
                 ).astype(added.dtype)
 
+                @pl.when(other == me)
+                def _():
+                    pltpu.make_async_copy(added.at[me], sums.at[me], own_sem).start()
+
                 @pl.when(other != me)
                 def _():
                     pltpu.make_async_remote_copy(
                         src_ref=added.at[other],
-                        dst_ref=sums_ref.at[me],
+                        dst_ref=sums.at[me],
                         send_sem=sum_send,
-                        recv_sem=sum_recv,
+                        recv_sem=sum_recv.at[my_group],
                         device_id=peer(other, core),
                         device_id_type=MESH,
                     ).start()
@@ -510,17 +518,32 @@
         def both(step, _):
             share(step)
             add(step - 1)
+            between(step - 1)
             return 0
 
         lax.fori_loop(1, some, both, 0)
         add(some - 1)
+        between(some - 1)
+
+    def feature_piece(piece):
+        count = own // PIECES
+        conv_back(grads, 0, pl.multiple_of(first_own + piece * count, 16), count)
+
+        def store(row, _):
+            grad[piece * (own_rows // PIECES) + row] = total[row_span(row), :].astype(grad.dtype)
+            return 0
+
+        lax.fori_loop(0, own_rows // PIECES, store, 0)
+        give_back(grad, grad_out, grad_send, grad_recv, piece, True)
+
+    def relit_piece(piece):
+        give_back(relit, relit_out, relit_send, relit_recv, piece, True)
 
     each_chunk(lambda start: conv(feats, 0, start), end_first)
     each_chunk(lambda start: conv(hidden, depth, start), end_second)
     kernel_grad(hidden, depth)
-    send_grad(groups // 2)
-    give_back(relit, relit_out, relit_send, relit_recv, True)
-    each_chunk(lambda start: conv_back(grads, depth, start), end_grad)
+    send_grad(groups // 2, relit_piece)
+    each_chunk(lambda start: conv_back(grads, depth, start, chunk), end_grad)
 
     def place_grad(row, _):
         spread(grads, row, slope[row_span(row), :])
@@ -528,14 +551,7 @@
 
     lax.fori_loop(0, rows, place_grad, 0)
     kernel_grad(feats, 0)
-    send_grad(0)
-    each_chunk(
-        lambda start: conv_back(grads, 0, start),
-        lambda row, back: store_own(grad, row, back),
-    )
-    give_back(grad, grad_out, grad_send, grad_recv, True)
-    last = pltpu.make_async_copy(added.at[me], sums_ref.at[me], own_sem)
-    last.start()
+    send_grad(0, feature_piece)
 
     def finish(group, _):
         to_sibling(group).wait_send()
@@ -547,14 +563,46 @@
     await_bytes(arrived, code_send)
     swap_copies(feat_ref, feat, feat_send, feat_recv, False)
     swap_copies(up_ref, up, up_send, up_recv, False)
-    give_back(relit, relit_out, relit_send, relit_recv, False)
-    give_back(grad, grad_out, grad_send, grad_recv, False)
-    for slot in range(2):
-        await_bytes(relit_out.at[slot], relit_recv.at[slot])
-        await_bytes(grad_out.at[slot], grad_recv.at[slot])
-    last.wait()
+
+    def finish_piece(piece, _):
+        give_back(relit, relit_out, relit_send, relit_recv, piece, False)
+        give_back(grad, grad_out, grad_send, grad_recv, piece, False)
+        return 0
+
+    lax.fori_loop(0, PIECES, finish_piece, 0)
+
+    def widen(group):
+        def block(slot, _):
+            chip = group * GROUP + slot
+            table[pl.ds(pl.multiple_of(chip * 40, 8), block_rows), :] = sums[chip].astype(
+                jnp.float32
+            )
+            return 0
+
+        lax.fori_loop(0, GROUP, block, 0)
+
+    pltpu.make_async_copy(added.at[me], sums.at[me], own_sem).wait()
+    await_bytes(sums.at[pl.ds(0, GROUP - 1)], sum_recv.at[my_group])
+    widen(my_group)
+
+    def take_sums(step, _):
+        group = lax.rem(my_group + groups - step, groups)
+        await_bytes(sums.at[pl.ds(0, GROUP)], sum_recv.at[group])
+        widen(group)
+        return 0
+
+    lax.fori_loop(1, groups, take_sums, 0)
+    for row in range(taps):
+        for side in range(2):
+            at = (2 * row + side) * LANES
+            summed_out[:, at : at + LANES] = table[
+                pl.ds(side * taps + row, chips, stride=40), :
+            ].astype(summed_out.dtype)
     await_bytes(added.at[pl.ds(0, chips - 1)], sum_send)
-    await_bytes(sums_ref.at[pl.ds(0, chips - 1)], sum_recv)
+    piece_rows = own_rows // PIECES
+    for slot in range(PIECES):
+        await_bytes(relit_out.at[0, pl.ds(0, piece_rows)], relit_recv.at[slot])
+        await_bytes(grad_out.at[0, pl.ds(0, piece_rows)], grad_recv.at[slot])
 
 
 def whole(scale, lights, codes, hyper_weight, features, upstream):
@@ -577,12 +625,12 @@
         functools.partial(whole_kernel, scale, lights),
         out_shape=(
             jax.ShapeDtypeStruct((chips, width), jnp.bfloat16),
-            jax.ShapeDtypeStruct((chips, block_rows, LANES), jnp.bfloat16),
+            jax.ShapeDtypeStruct((chips, own_len), jnp.bfloat16),
             image,
             image,
         ),
         in_specs=[vmem, anywhere, anywhere, anywhere],
-        out_specs=(vmem, anywhere, anywhere, anywhere),
+        out_specs=(vmem, vmem, anywhere, anywhere),
         scratch_shapes=[
             pltpu.VMEM((width, own_len), jnp.bfloat16),
             pltpu.VMEM((8 * lights, LANES), jnp.float32),
@@ -598,9 +646,10 @@
             shifted,
             shifted,
             pltpu.VMEM((frame, channels), jnp.float32),
-            pltpu.VMEM((9 * columns, channels), jnp.float32),
+            pltpu.VMEM((CHUNK_ROWS * columns, channels), jnp.float32),
             pltpu.VMEM((own_rows, columns, channels), jnp.bfloat16),
             pltpu.VMEM((own_rows, columns, channels), jnp.bfloat16),
+            block,
             block,
             block,
             block,
@@ -619,11 +668,11 @@
             dma((groups,)),
             dma((groups,)),
             dma,
-            dma,
-            dma((2,)),
-            dma((2,)),
-            dma((2,)),
-            dma((2,)),
+            dma((groups,)),
+            dma((PIECES,)),
+            dma((PIECES,)),
+            dma((PIECES,)),
+            dma((PIECES,)),
         ],
         compiler_params=pltpu.CompilerParams(
             has_side_effects=True, collective_id=0, vmem_limit_bytes=VMEM
@@ -631,12 +680,60 @@
     )(codes, hyper_weight, features, upstream)
 
 
+def last_kernel(
+    scale, codes_ref, summed_ref, relit_ref, grad_ref, hyper_out, relit_out, grad_out, ready, sems, out_sems
+):
+    copies = [
+        pltpu.make_async_copy(relit_ref, relit_out, sems.at[0]),
+        pltpu.make_async_copy(grad_ref, grad_out, sems.at[1]),
+    ]
+    for copy in copies:
+        copy.start()
+    codes = codes_ref[...].T
+    steps = ready.shape[0]
+    width = ready.shape[2]
+    for step in range(steps):
+        span = pl.ds(step * width, width)
+        ready[step] = (
+            scale * jnp.dot(codes, summed_ref[:, span], preferred_element_type=jnp.float32)
+        ).astype(ready.dtype)
+        copy = pltpu.make_async_copy(ready.at[step], hyper_out.at[:, span], out_sems.at[step])
+        copy.start()
+        copies.append(copy)
+    for copy in copies:
+        copy.wait()
+
+
+def last_step(scale, codes, summed, relit, feature_grad):
+    chips, depth = codes.shape
+    own_len = summed.shape[1]
+    steps = 9
+    anywhere = pl.BlockSpec(memory_space=pl.ANY)
+    vmem = pl.BlockSpec(memory_space=pltpu.VMEM)
+    return pl.pallas_call(
+        functools.partial(last_kernel, scale),
+        out_shape=(
+            jax.ShapeDtypeStruct((depth, own_len), jnp.bfloat16),
+            jax.ShapeDtypeStruct(relit.shape, jnp.bfloat16),
+            jax.ShapeDtypeStruct(feature_grad.shape, jnp.bfloat16),
+        ),
+        in_specs=[vmem, vmem, anywhere, anywhere],
+        out_specs=(anywhere,) * 3,
+        scratch_shapes=[
+            pltpu.VMEM((steps, depth, own_len // steps), jnp.bfloat16),
+            pltpu.SemaphoreType.DMA((2,)),
+            pltpu.SemaphoreType.DMA((steps,)),
+        ],
+        compiler_params=pltpu.CompilerParams(vmem_limit_bytes=VMEM),
+    )(codes, summed, relit, feature_grad)
+
+
 def shards(light_ids, tile_offsets, light_table, hyper_weight, features, upstream_grad):
     channels = features.shape[3]
     scale = 1.0 / math.sqrt(9 * channels)
     lights = lax.axis_size("light")
     own_codes = light_codes(light_ids, tile_offsets, light_table)
-    codes, sums, relit, feature_grad = whole(
+    codes, summed, relit, feature_grad = whole(
         scale,
         lights,
         own_codes.astype(jnp.float32).reshape(8, LANES),
@@ -644,14 +741,7 @@
         features,
         upstream_grad,
     )
-    chips = 2 * lights
-    taps = hyper_weight.shape[1] // channels
-    summed = (
-        sums.reshape(chips, 2, taps, LANES).transpose(0, 2, 1, 3).reshape(chips, taps * channels)
-    )
-    hyper_grad = (
-        scale * jnp.einsum("lz,ls->zs", codes, summed, preferred_element_type=jnp.float32)
-    ).astype(jnp.bfloat16)
+    hyper_grad, relit, feature_grad = last_step(scale, codes, summed, relit, feature_grad)
     return (relit, feature_grad, hyper_grad)
 
 

time: 120 us -> 161 us (1.34)
  Pallas kernels: 109 us -> 158 us
  local copies, waits for them, and re-layouts: 4.87 us -> 0.74 us
  matrix products: 4.56 us -> 0.95 us
    pallas_call x0 -> x1, Pallas kernels: none -> 50.2 us  [last_step(): pl.pallas_call(functools.partial(last_kernel, scale), out_shape=(jax.Shap...]
    dot_general x1 -> x0, matrix products: 3.61 us -> none  [shards(): jnp.einsum('lz,ls->zs', codes, summed, preferred_element_type=jnp.float32)]
    unnamed x10 -> x2, local copies, waits for them, and re-layouts: 1.9 us -> 0.13 us
    pallas_call x1 -> x0, local copies, waits for them, and re-layouts: 1.62 us -> none  [whole(): pl.pallas_call(functools.partial(whole_kernel, scale, lights), out_shape=...]
where the time goes in v5:
time: 161 us
  Pallas kernels  158 us (98%)
    pallas_call x1, Pallas kernels, whole(): pl.pallas_call(functools.partial(whole_kernel, scale, lights), out_shape=...  108 us
    pallas_call x1, Pallas kernels, last_step(): pl.pallas_call(functools.partial(last_kernel, scale), out_shape=(jax.Shap...  50.2 us

profile of v5, /device:TPU:1, one launch (start us, length us, event | category | flops | bytes accessed | tf_op | source)
XLA Modules:
  0.0 161.0 jit_solution(6155302350897795499)
XLA Ops:
  0.6 0.0 copy-start
  0.6 0.7 convert_element_type.8
  1.4 0.1 multiply_sine_fusion
  1.5 0.1 copy-done
  1.6 1.0 multiply_reduce_fusion
  2.6 0.1 fusion.2
  2.6 0.6 reshape.29.codes_ref
  3.3 107.6 %shard_map.85 = (bf16[128,512]{1,0:T(8,128)(2,1)}, bf16[128,4608]{1,0:T(8,128)(2,1)}, bf16[2,16,48,256]{3,2,1,0:T(8,128)(2,1)}, bf16[2,16,48,256]{3,2,1,0:T(8,128)(2,1)}) custom-call(f32[8,128]{1,0:T(8,128)} %reshape.29.codes_ref, bf16[512,4608]{1,0:T(8,128)(2,1)} %hyper_ref.1, bf16[2,16,48,256]{3,2,1,0:T(8,128)(2,1)} %feat_ref.1, ...), custom_call_target="tpu_custom_call" | custom-call | tf_op jit(solution)/shard_map/pallas_call | solution.py:624
  110.8 50.2 %shard_map.86 = (bf16[512,4608]{1,0:T(8,128)(2,1)}, bf16[2,16,48,256]{3,2,1,0:T(8,128)(2,1)}, bf16[2,16,48,256]{3,2,1,0:T(8,128)(2,1)}) custom-call(bf16[128,512]{1,0:T(8,128)(2,1)} %get-tuple-element.10.codes_ref, bf16[128,4608]{1,0:T(8,128)(2,1)} %get-tuple-element.11.summed_ref, bf16[2,16,48,256]{3,2,1,0:T(8,128)(2,1)} %get-tuple-element.12.relit_ref, ...), custom_call_target="tpu_custom_call" | custom-call | tf_op jit(solution)/shard_map/pallas_call | solution.py:713
  (2 shorter events, 0.0 us)
Async XLA Ops:
  0.6 1.0 copy-start

commit v6 on v5

--- a/solution.py
+++ b/solution.py
@@ -13,6 +13,7 @@
 GROUP = 16
 HALO = 4
 PIECES = 4
+AT_ONCE = 4
 CHUNK_ROWS = 18
 VMEM = 60 * 1024 * 1024
 
@@ -334,19 +335,22 @@
         )
 
     def gather(group, from_core):
-        def block(slot, _):
-            chip = group * GROUP + slot
-            line[...] = blocks[from_core, chip].astype(jnp.float32)
-
-            def move(side, _):
-                wide[side, pl.ds((2 * chip + from_core) * taps, taps), :] = line[
-                    pl.ds(side * taps, taps), :
-                ]
-                return 0
-
-            return lax.fori_loop(0, 2, move, 0)
-
-        lax.fori_loop(0, GROUP, block, 0)
+        def block(step, _):
+            several = [group * GROUP + step * AT_ONCE + k for k in range(AT_ONCE)]
+            for k, chip in enumerate(several):
+                line[k] = blocks[from_core, chip].astype(jnp.float32)
+            for k, chip in enumerate(several):
+
+                def move(side, _):
+                    wide[side, pl.ds((2 * chip + from_core) * taps, taps), :] = line[
+                        k, pl.ds(side * taps, taps), :
+                    ]
+                    return 0
+
+                lax.fori_loop(0, 2, move, 0)
+            return 0
+
+        lax.fori_loop(0, GROUP // AT_ONCE, block, 0)
 
     def end_group(group):
         to_sibling(group).wait_recv()
@@ -459,13 +463,27 @@
             device_id_type=MESH,
         )
 
-    def pick(owner):
-        def move(side, _):
-            line[pl.ds(side * taps, taps), :] = wide[side, pl.ds(owner * taps, taps), :]
-            return 0
-
-        lax.fori_loop(0, 2, move, 0)
-        return line[...]
+    def pick(slot, owner):
+        for side in range(2):
+            line[slot, side * taps : (side + 1) * taps, :] = wide[
+                side, pl.ds(owner * taps, taps), :
+            ]
+
+    def send_sum(other):
+        @pl.when(other == me)
+        def _():
+            pltpu.make_async_copy(added.at[me], sums.at[me], own_sem).start()
+
+        @pl.when(other != me)
+        def _():
+            pltpu.make_async_remote_copy(
+                src_ref=added.at[other],
+                dst_ref=sums.at[me],
+                send_sem=sum_send,
+                recv_sem=sum_recv.at[my_group],
+                device_id=peer(other, core),
+                device_id_type=MESH,
+            ).start()
 
     def send_grad(first, between):
         some = groups // 2
@@ -476,42 +494,37 @@
         def share(step):
             group = group_at(step)
 
-            def block(slot, _):
-                chip = group * GROUP + slot
-                parts[chip] = pick(2 * chip + 1 - core).astype(parts.dtype)
+            def block(step, _):
+                several = [group * GROUP + step * AT_ONCE + k for k in range(AT_ONCE)]
+                for k, chip in enumerate(several):
+                    pick(k, 2 * chip + 1 - core)
+                for k, chip in enumerate(several):
+                    parts[chip] = line[k].astype(parts.dtype)
                 return 0
 
-            lax.fori_loop(0, GROUP, block, 0)
+            lax.fori_loop(0, GROUP // AT_ONCE, block, 0)
             part_copy(group).start()
 
         def add(step):
             group = group_at(step)
             part_copy(group).wait_recv()
 
-            def block(slot, _):
-                other = group * GROUP + lax.rem(my_slot + slot, GROUP)
-                added[other] = (
-                    pick(2 * other + core) + theirs[other].astype(jnp.float32)
-                ).astype(added.dtype)
-
-                @pl.when(other == me)
-                def _():
-                    pltpu.make_async_copy(added.at[me], sums.at[me], own_sem).start()
-
-                @pl.when(other != me)
-                def _():
-                    pltpu.make_async_remote_copy(
-                        src_ref=added.at[other],
-                        dst_ref=sums.at[me],
-                        send_sem=sum_send,
-                        recv_sem=sum_recv.at[my_group],
-                        device_id=peer(other, core),
-                        device_id_type=MESH,
-                    ).start()
-
+            def block(step, _):
+                several = [
+                    group * GROUP + lax.rem(my_slot + step * AT_ONCE + k, GROUP)
+                    for k in range(AT_ONCE)
+                ]
+                for k, other in enumerate(several):
+                    pick(k, 2 * other + core)
+                for k, other in enumerate(several):
+                    added[other] = (line[k] + theirs[other].astype(jnp.float32)).astype(
+                        added.dtype
+                    )
+                for other in several:
+                    send_sum(other)
                 return 0
 
-            lax.fori_loop(0, GROUP, block, 0)
+            lax.fori_loop(0, GROUP // AT_ONCE, block, 0)
 
         share(0)
 
@@ -536,13 +549,15 @@
         lax.fori_loop(0, own_rows // PIECES, store, 0)
         give_back(grad, grad_out, grad_send, grad_recv, piece, True)
 
-    def relit_piece(piece):
+    def relit_piece(piece, _):
         give_back(relit, relit_out, relit_send, relit_recv, piece, True)
+        return 0
 
     each_chunk(lambda start: conv(feats, 0, start), end_first)
     each_chunk(lambda start: conv(hidden, depth, start), end_second)
+    lax.fori_loop(0, PIECES, relit_piece, 0)
     kernel_grad(hidden, depth)
-    send_grad(groups // 2, relit_piece)
+    send_grad(groups // 2, lambda step: None)
     each_chunk(lambda start: conv_back(grads, depth, start, chunk), end_grad)
 
     def place_grad(row, _):
@@ -638,7 +653,7 @@
             block,
             pltpu.VMEM((2, chips, block_rows, LANES), jnp.bfloat16),
             pltpu.VMEM((2, 2 * depth, LANES), jnp.float32),
-            pltpu.VMEM((block_rows, LANES), jnp.float32),
+            pltpu.VMEM((AT_ONCE, block_rows, LANES), jnp.float32),
             pltpu.VMEM((2 * depth, channels), jnp.bfloat16),
             pltpu.VMEM((rows, columns, channels), jnp.bfloat16),
             pltpu.VMEM((rows, columns, channels), jnp.bfloat16),
@@ -681,17 +696,35 @@
 
 
 def last_kernel(
-    scale, codes_ref, summed_ref, relit_ref, grad_ref, hyper_out, relit_out, grad_out, ready, sems, out_sems
+    scale,
+    codes_ref,
+    summed_ref,
+    relit_ref,
+    grad_ref,
+    hyper_out,
+    relit_out,
+    grad_out,
+    relit,
+    grad,
+    ready,
+    in_sems,
+    image_sems,
+    out_sems,
 ):
-    copies = [
-        pltpu.make_async_copy(relit_ref, relit_out, sems.at[0]),
-        pltpu.make_async_copy(grad_ref, grad_out, sems.at[1]),
+    loads = [
+        pltpu.make_async_copy(relit_ref, relit, in_sems.at[0]),
+        pltpu.make_async_copy(grad_ref, grad, in_sems.at[1]),
     ]
-    for copy in copies:
-        copy.start()
+    stores = [
+        pltpu.make_async_copy(relit, relit_out, image_sems.at[0]),
+        pltpu.make_async_copy(grad, grad_out, image_sems.at[1]),
+    ]
+    for load in loads:
+        load.start()
     codes = codes_ref[...].T
     steps = ready.shape[0]
     width = ready.shape[2]
+    pending = []
     for step in range(steps):
         span = pl.ds(step * width, width)
         ready[step] = (
@@ -699,8 +732,11 @@
         ).astype(ready.dtype)
         copy = pltpu.make_async_copy(ready.at[step], hyper_out.at[:, span], out_sems.at[step])
         copy.start()
-        copies.append(copy)
-    for copy in copies:
+        pending.append(copy)
+        if step in (2, 4):
+            loads[step // 2 - 1].wait()
+            stores[step // 2 - 1].start()
+    for copy in pending + stores:
         copy.wait()
 
 
@@ -720,7 +756,10 @@
         in_specs=[vmem, vmem, anywhere, anywhere],
         out_specs=(anywhere,) * 3,
         scratch_shapes=[
+            pltpu.VMEM(relit.shape, jnp.bfloat16),
+            pltpu.VMEM(feature_grad.shape, jnp.bfloat16),
             pltpu.VMEM((steps, depth, own_len // steps), jnp.bfloat16),
+            pltpu.SemaphoreType.DMA((2,)),
             pltpu.SemaphoreType.DMA((2,)),
             pltpu.SemaphoreType.DMA((steps,)),
         ],

time: 161 us -> 113 us (0.70)
  Pallas kernels: 158 us -> 109 us
    pallas_call x1, Pallas kernels: 50.2 us -> 4.79 us  [last_step(): pl.pallas_call(functools.partial(last_kernel, scale), out_shape=(jax.Shap...]
    pallas_call x1, Pallas kernels: 108 us -> 105 us  [whole(): pl.pallas_call(functools.partial(whole_kernel, scale, lights), out_shape=...]
where the time goes in v6:
time: 113 us
  Pallas kernels  109 us (96%)
    pallas_call x1, Pallas kernels, whole(): pl.pallas_call(functools.partial(whole_kernel, scale, lights), out_shape=...  105 us
    pallas_call x1, Pallas kernels, last_step(): pl.pallas_call(functools.partial(last_kernel, scale), out_shape=(jax.Shap...  4.79 us

profile of v6, /device:TPU:1, one launch (start us, length us, event | category | flops | bytes accessed | tf_op | source)
XLA Modules:
  0.0 112.6 jit_solution(9025235563544661393)
XLA Ops:
  0.6 0.0 copy-start
  0.6 0.7 convert_element_type.8
  1.4 0.1 multiply_sine_fusion
  1.5 0.1 copy-done
  1.6 1.0 multiply_reduce_fusion
  2.6 0.1 fusion.2
  2.6 0.6 reshape.29.codes_ref
  3.3 104.6 %shard_map.85 = (bf16[128,512]{1,0:T(8,128)(2,1)}, bf16[128,4608]{1,0:T(8,128)(2,1)}, bf16[2,16,48,256]{3,2,1,0:T(8,128)(2,1)}, bf16[2,16,48,256]{3,2,1,0:T(8,128)(2,1)}) custom-call(f32[8,128]{1,0:T(8,128)} %reshape.29.codes_ref, bf16[512,4608]{1,0:T(8,128)(2,1)} %hyper_ref.1, bf16[2,16,48,256]{3,2,1,0:T(8,128)(2,1)} %feat_ref.1, ...), custom_call_target="tpu_custom_call" | custom-call | tf_op jit(solution)/shard_map/pallas_call | solution.py:639
  107.8 4.8 %shard_map.86 = (bf16[512,4608]{1,0:T(8,128)(2,1)}, bf16[2,16,48,256]{3,2,1,0:T(8,128)(2,1)}, bf16[2,16,48,256]{3,2,1,0:T(8,128)(2,1)}) custom-call(bf16[128,512]{1,0:T(8,128)(2,1)} %get-tuple-element.10.codes_ref, bf16[128,4608]{1,0:T(8,128)(2,1)} %get-tuple-element.11.summed_ref, bf16[2,16,48,256]{3,2,1,0:T(8,128)(2,1)} %get-tuple-element.12.relit_ref, ...), custom_call_target="tpu_custom_call" | custom-call | tf_op jit(solution)/shard_map/pallas_call | solution.py:749
  (2 shorter events, 0.0 us)
Async XLA Ops:
  0.6 1.0 copy-start

commit v7 on v6

--- a/solution.py
+++ b/solution.py
@@ -10,7 +10,8 @@
 
 MESH = pl.DeviceIdType.MESH
 LANES = 128
-GROUP = 16
+GROUP = 8
+LINE = 8
 HALO = 4
 PIECES = 4
 AT_ONCE = 4
@@ -42,22 +43,29 @@
     return (chip // 2, (chip % 2) * 2 + core)
 
 
+def line_peer(light, step):
+    return light - light % LINE + lax.rem(light % LINE + step, LINE)
+
+
+def plane_peer(light, step):
+    return lax.rem(light + step * LINE, lax.axis_size("light"))
+
+
 def greet():
-    light, half, core, me = place()
-    chips = 2 * lax.axis_size("light")
+    light, tex = lax.axis_index("light"), lax.axis_index("tex")
+    lines = lax.axis_size("light") // LINE
     barrier = pltpu.get_barrier_semaphore()
 
     def signal(target):
         pl.semaphore_signal(barrier, inc=1, device_id=target, device_id_type=MESH)
 
-    def signal_chip(step, _):
-        signal(peer(lax.rem(me + step, chips), core))
-        return 0
-
-    lax.fori_loop(1, chips, signal_chip, 0)
-    signal((light, half * 2 + 1 - core))
-    signal((light, (1 - half) * 2 + 1 - core))
-    pl.semaphore_wait(barrier, chips + 1)
+    for step in range(1, LINE):
+        signal((line_peer(light, step), tex))
+    for step in range(1, lines):
+        signal((plane_peer(light, step), tex))
+    for step in range(1, 4):
+        signal((light, lax.rem(tex + step, 4)))
+    pl.semaphore_wait(barrier, LINE + lines + 1)
 
 
 def await_bytes(ref, sem):
@@ -201,6 +209,8 @@
     hyper_sem,
     code_send,
     code_recv,
+    line_send,
+    line_recv,
     own_sem,
     block_send,
     block_recv,
@@ -240,28 +250,41 @@
     greet()
 
     mine = pl.ds(pl.multiple_of(light * 8, 8), 8)
-    codes[mine, :] = codes_ref[...]
-
-    def send_codes(step, _):
+    codes[mine, :] = jnp.concatenate(
+        [
+            codes_ref[row : row + 1, k * LANES : (k + 1) * LANES]
+            for row in range(2)
+            for k in range(4)
+        ],
+        axis=0,
+    )
+    lines = lights // LINE
+    whole_line = pl.ds(pl.multiple_of(light // LINE * (8 * LINE), 8 * LINE), 8 * LINE)
+
+    def code_copy(span, target, send, recv):
         pltpu.make_async_remote_copy(
-            src_ref=codes_ref,
-            dst_ref=codes.at[mine],
-            send_sem=code_send,
-            recv_sem=code_recv,
-            device_id=(lax.rem(light + step, lights), half * 2 + core),
+            src_ref=codes.at[span],
+            dst_ref=codes.at[span],
+            send_sem=send,
+            recv_sem=recv,
+            device_id=(target, half * 2 + core),
             device_id_type=MESH,
         ).start()
-        return 0
-
-    lax.fori_loop(1, lights, send_codes, 0)
+
+    for step in range(1, LINE):
+        code_copy(mine, line_peer(light, step), code_send, code_recv)
     swap_copies(feat_ref, feat, feat_send, feat_recv, True)
     swap_copies(up_ref, up, up_send, up_recv, True)
     for image in (feats, hidden, grads):
         edge = jnp.zeros((columns, image.shape[1]), image.dtype)
         image[:columns] = edge
         image[frame + columns :] = edge
-    arrived = codes.at[pl.ds(0, 8 * (lights - 1))]
-    await_bytes(arrived, code_recv)
+    near = codes.at[pl.ds(0, 8 * (LINE - 1))]
+    far = codes.at[pl.ds(0, 8 * LINE * (lines - 1))]
+    await_bytes(near, code_recv)
+    for step in range(1, lines):
+        code_copy(whole_line, plane_peer(light, step), line_send, line_recv)
+    await_bytes(far, line_recv)
     all_codes = jnp.concatenate(
         [codes[pl.ds(k, chips, stride=4), :] for k in range(4)], axis=1
     ).astype(jnp.bfloat16)
@@ -538,7 +561,14 @@
         add(some - 1)
         between(some - 1)
 
-    def feature_piece(piece):
+    def feature_piece(step):
+        every = groups // 2 // PIECES
+
+        @pl.when(step % every == every - 1)
+        def _():
+            feature_rows(step // every)
+
+    def feature_rows(piece):
         count = own // PIECES
         conv_back(grads, 0, pl.multiple_of(first_own + piece * count, 16), count)
 
@@ -575,7 +605,8 @@
 
     lax.fori_loop(0, groups, finish, 0)
     await_bytes(ready.at[pl.ds(0, chips - 1)], block_send)
-    await_bytes(arrived, code_send)
+    await_bytes(near, code_send)
+    await_bytes(far, line_send)
     swap_copies(feat_ref, feat, feat_send, feat_recv, False)
     swap_copies(up_ref, up, up_send, up_recv, False)
 
@@ -673,6 +704,8 @@
             dma,
             dma,
             dma,
+            dma,
+            dma,
             dma((groups,)),
             dma((groups,)),
             dma((groups,)),
@@ -775,7 +808,7 @@
     codes, summed, relit, feature_grad = whole(
         scale,
         lights,
-        own_codes.astype(jnp.float32).reshape(8, LANES),
+        own_codes.astype(jnp.float32),
         hyper_weight,
         features,
         upstream_grad,

time: 113 us -> 124 us (1.097)
  Pallas kernels: 109 us -> 120 us
    pallas_call x1, Pallas kernels: 105 us -> 115 us  [whole(): pl.pallas_call(functools.partial(whole_kernel, scale, lights), out_shape=...]
where the time goes in v7:
time: 124 us; the launch traced here: 123 us
  Pallas kernels  120 us (97%)
  other arithmetic  1.51 us (1%)
    pallas_call x1, Pallas kernels, whole(): pl.pallas_call(functools.partial(whole_kernel, scale, lights), out_shape=...  115 us
    pallas_call x1, Pallas kernels, last_step(): pl.pallas_call(functools.partial(last_kernel, scale), out_shape=(jax.Shap...  4.79 us

profile of v7, /device:TPU:1, one launch (start us, length us, event | category | flops | bytes accessed | tf_op | source)
XLA Modules:
  0.0 123.3 jit_solution(9089946850125962537)
XLA Ops:
  0.6 0.0 copy-start
  0.6 0.7 convert_element_type.10
  1.4 0.1 multiply_sine_fusion
  1.5 0.1 copy-done
  1.6 1.0 multiply_reduce_fusion
  2.6 0.7 fusion.2.codes_ref
  3.2 115.3 %shard_map.85 = (bf16[128,512]{1,0:T(8,128)(2,1)}, bf16[128,4608]{1,0:T(8,128)(2,1)}, bf16[2,16,48,256]{3,2,1,0:T(8,128)(2,1)}, bf16[2,16,48,256]{3,2,1,0:T(8,128)(2,1)}) custom-call(f32[2,512]{1,0:T(2,128)} %fusion.2.codes_ref, bf16[512,4608]{1,0:T(8,128)(2,1)} %hyper_ref.1, bf16[2,16,48,256]{3,2,1,0:T(8,128)(2,1)} %feat_ref.1, bf16[2,16,48,256]{3,2,1,0:T(8,128)(2,1)} %up_ref.1), custom_call_target="tpu_custom_call" | custom-call | tf_op jit(solution)/shard_map/pallas_call | solution.py:670
  118.5 4.8 %shard_map.86 = (bf16[512,4608]{1,0:T(8,128)(2,1)}, bf16[2,16,48,256]{3,2,1,0:T(8,128)(2,1)}, bf16[2,16,48,256]{3,2,1,0:T(8,128)(2,1)}) custom-call(bf16[128,512]{1,0:T(8,128)(2,1)} %get-tuple-element.10.codes_ref, bf16[128,4608]{1,0:T(8,128)(2,1)} %get-tuple-element.11.summed_ref, bf16[2,16,48,256]{3,2,1,0:T(8,128)(2,1)} %get-tuple-element.12.relit_ref, ...), custom_call_target="tpu_custom_call" | custom-call | tf_op jit(solution)/shard_map/pallas_call | solution.py:782
  (2 shorter events, 0.0 us)
Async XLA Ops:
  0.6 1.0 copy-start

commit v8 on v7

--- a/solution.py
+++ b/solution.py
@@ -10,7 +10,7 @@
 
 MESH = pl.DeviceIdType.MESH
 LANES = 128
-GROUP = 8
+GROUP = 16
 LINE = 8
 HALO = 4
 PIECES = 4

time: 124 us -> 125 us (level)
    pallas_call x1, Pallas kernels: 115 us -> 117 us  [whole(): pl.pallas_call(functools.partial(whole_kernel, scale, lights), out_shape=...]
where the time goes in v8:
time: 125 us
  Pallas kernels  121 us (97%)
  other arithmetic  1.51 us (1%)
    pallas_call x1, Pallas kernels, whole(): pl.pallas_call(functools.partial(whole_kernel, scale, lights), out_shape=...  117 us
    pallas_call x1, Pallas kernels, last_step(): pl.pallas_call(functools.partial(last_kernel, scale), out_shape=(jax.Shap...  4.79 us

profile of v8, /device:TPU:1, one launch (start us, length us, event | category | flops | bytes accessed | tf_op | source)
XLA Modules:
  0.0 124.7 jit_solution(16706600755649897392)
XLA Ops:
  0.6 0.0 copy-start
  0.6 0.7 convert_element_type.10
  1.4 0.1 multiply_sine_fusion
  1.5 0.1 copy-done
  1.6 1.0 multiply_reduce_fusion
  2.6 0.7 fusion.2.codes_ref
  3.2 116.6 %shard_map.85 = (bf16[128,512]{1,0:T(8,128)(2,1)}, bf16[128,4608]{1,0:T(8,128)(2,1)}, bf16[2,16,48,256]{3,2,1,0:T(8,128)(2,1)}, bf16[2,16,48,256]{3,2,1,0:T(8,128)(2,1)}) custom-call(f32[2,512]{1,0:T(2,128)} %fusion.2.codes_ref, bf16[512,4608]{1,0:T(8,128)(2,1)} %hyper_ref.1, bf16[2,16,48,256]{3,2,1,0:T(8,128)(2,1)} %feat_ref.1, bf16[2,16,48,256]{3,2,1,0:T(8,128)(2,1)} %up_ref.1), custom_call_target="tpu_custom_call" | custom-call | tf_op jit(solution)/shard_map/pallas_call | solution.py:670
  119.9 4.8 %shard_map.86 = (bf16[512,4608]{1,0:T(8,128)(2,1)}, bf16[2,16,48,256]{3,2,1,0:T(8,128)(2,1)}, bf16[2,16,48,256]{3,2,1,0:T(8,128)(2,1)}) custom-call(bf16[128,512]{1,0:T(8,128)(2,1)} %get-tuple-element.10.codes_ref, bf16[128,4608]{1,0:T(8,128)(2,1)} %get-tuple-element.11.summed_ref, bf16[2,16,48,256]{3,2,1,0:T(8,128)(2,1)} %get-tuple-element.12.relit_ref, ...), custom_call_target="tpu_custom_call" | custom-call | tf_op jit(solution)/shard_map/pallas_call | solution.py:782
  (2 shorter events, 0.0 us)
Async XLA Ops:
  0.6 1.0 copy-start

commit v9 on v8

--- a/solution.py
+++ b/solution.py
@@ -273,8 +273,6 @@
 
     for step in range(1, LINE):
         code_copy(mine, line_peer(light, step), code_send, code_recv)
-    swap_copies(feat_ref, feat, feat_send, feat_recv, True)
-    swap_copies(up_ref, up, up_send, up_recv, True)
     for image in (feats, hidden, grads):
         edge = jnp.zeros((columns, image.shape[1]), image.dtype)
         image[:columns] = edge
@@ -324,6 +322,8 @@
         return 0
 
     lax.fori_loop(1, chips, send_block, 0)
+    swap_copies(feat_ref, feat, feat_send, feat_recv, True)
+    swap_copies(up_ref, up, up_send, up_recv, True)
 
     def row_span(row):
         return pl.ds(pl.multiple_of(row * columns, 16), columns)
@@ -337,14 +337,11 @@
         image[span, channels : 2 * channels] = values.astype(image.dtype)
         image[span, 2 * channels :] = after.astype(image.dtype)
 
-    swap_arrivals(feat_ref, feat, feat_recv)
-    swap_arrivals(up_ref, up, up_recv)
 
     def place_feats(row, _):
         spread(feats, row, feat[row].astype(jnp.float32))
         return 0
 
-    lax.fori_loop(0, rows, place_feats, 0)
 
     def to_sibling(group):
         span = blocks.at[core, pl.ds(group * GROUP, GROUP)]
@@ -397,6 +394,9 @@
         return 0
 
     lax.fori_loop(1, groups, take_group, 0)
+    swap_arrivals(feat_ref, feat, feat_recv)
+    swap_arrivals(up_ref, up, up_recv)
+    lax.fori_loop(0, rows, place_feats, 0)
     end_group(lax.rem(my_group + 1, groups))
 
     def conv(image, base, start):

time: 125 us -> 113 us (0.904)
  Pallas kernels: 121 us -> 109 us
    pallas_call x1, Pallas kernels: 117 us -> 104 us  [whole(): pl.pallas_call(functools.partial(whole_kernel, scale, lights), out_shape=...]
where the time goes in v9:
time: 113 us; the launch traced here: 112 us
  Pallas kernels  109 us (96%)
  other arithmetic  1.51 us (1%)
    pallas_call x1, Pallas kernels, whole(): pl.pallas_call(functools.partial(whole_kernel, scale, lights), out_shape=...  104 us
    pallas_call x1, Pallas kernels, last_step(): pl.pallas_call(functools.partial(last_kernel, scale), out_shape=(jax.Shap...  4.79 us

profile of v9, /device:TPU:1, one launch (start us, length us, event | category | flops | bytes accessed | tf_op | source)
XLA Modules:
  0.0 112.4 jit_solution(16453316671774550058)
XLA Ops:
  0.6 0.0 copy-start
  0.6 0.7 convert_element_type.10
  1.4 0.1 multiply_sine_fusion
  1.5 0.1 copy-done
  1.6 1.0 multiply_reduce_fusion
  2.6 0.7 fusion.2.codes_ref
  3.2 104.4 %shard_map.85 = (bf16[128,512]{1,0:T(8,128)(2,1)}, bf16[128,4608]{1,0:T(8,128)(2,1)}, bf16[2,16,48,256]{3,2,1,0:T(8,128)(2,1)}, bf16[2,16,48,256]{3,2,1,0:T(8,128)(2,1)}) custom-call(f32[2,512]{1,0:T(2,128)} %fusion.2.codes_ref, bf16[512,4608]{1,0:T(8,128)(2,1)} %hyper_ref.1, bf16[2,16,48,256]{3,2,1,0:T(8,128)(2,1)} %feat_ref.1, bf16[2,16,48,256]{3,2,1,0:T(8,128)(2,1)} %up_ref.1), custom_call_target="tpu_custom_call" | custom-call | tf_op jit(solution)/shard_map/pallas_call | solution.py:670
  107.6 4.8 %shard_map.86 = (bf16[512,4608]{1,0:T(8,128)(2,1)}, bf16[2,16,48,256]{3,2,1,0:T(8,128)(2,1)}, bf16[2,16,48,256]{3,2,1,0:T(8,128)(2,1)}) custom-call(bf16[128,512]{1,0:T(8,128)(2,1)} %get-tuple-element.10.codes_ref, bf16[128,4608]{1,0:T(8,128)(2,1)} %get-tuple-element.11.summed_ref, bf16[2,16,48,256]{3,2,1,0:T(8,128)(2,1)} %get-tuple-element.12.relit_ref, ...), custom_call_target="tpu_custom_call" | custom-call | tf_op jit(solution)/shard_map/pallas_call | solution.py:782
  (2 shorter events, 0.0 us)
Async XLA Ops:
  0.6 1.0 copy-start
